TPU v7x, 32 devices: a whole 2x2x4 slice. The times are simulated.
32 devices in a mesh: row: 8 (over y, x, core), rep: 4 (over z).
Axes of the slice: x: 2, y: 2, z: 4, core: 2. Of those that a mesh axis runs over, the one named last changes fastest.
Arguments:
- node_feats: bfloat16 [8192, 1024], P('row'), may hold values from -6 to 6
- block_cols: int32 [64, 4], P('row'), may hold values from -1 to 63, as said below
- block_vals: bfloat16 [64, 4, 128, 128], P('row'), may hold values from -0.26367188 to 0.26367188
- w_in: bfloat16 [1024, 4096], P(None, 'rep'), may hold values from -0.1875 to 0.1875
- w_out: bfloat16 [1024, 4096], P(None, 'rep'), may hold values from -0.09375 to 0.09375
- cotangent: bfloat16 [8192, 1024], P('row', 'rep'), may hold values from -6 to 6
Outputs:
- updated: bfloat16 [8192, 1024], P('row', 'rep')
- grad_nodes: bfloat16 [8192, 1024], P('row', 'rep')
Inputs may be any that keep to these rules, and one draw needn't show every extreme that they name: `block_cols`: slot 0 of block-row b holds b itself. Every other present block-column lies within 16 block-rows of its block-row; absent slots hold -1, and the number of present blocks differs from block-row to block-row. A pair of block-row and block-column may repeat.
All inputs are finite; a program needn't handle non-finite values.
Results may differ from a plain program's by a relative error of at most 0.013.
Values may be sent and summed in bfloat16 or wider, within the bound.
A program may use at most 128 MiB of HBM per device.

v0:
```python
import functools

import jax
import jax.numpy as jnp
from jax import lax
from jax.experimental import pallas as pl
from jax.experimental.pallas import tpu as pltpu
from jax.sharding import PartitionSpec as P

F32 = jnp.float32
BF16 = jnp.bfloat16
MESH = pl.DeviceIdType.MESH


def dot(a, b, dims=((1,), (0,))):
    return lax.dot_general(a, b, (dims, ((), ())), preferred_element_type=F32)


def gelu_pair(v):
    c = 0.7978845608
    vv = v * v
    t = jnp.tanh(c * (v + 0.044715 * v * vv))
    half = 0.5 * (1.0 + t)
    value = v * half
    slope = half + 0.5 * v * (1.0 - t * t) * c * (1.0 + 3.0 * 0.044715 * vv)
    return value, slope


def kernel(
    n_row, n_rep, mask_ref, feats_ref, vals_ref, w_in_ref, w_out_ref, cot_ref,
    upd_ref, grad_ref,
    ext, vals_t, dense, dense_t, agg_acc, w2_in, w2_out, cot_full, agg, agg_full, hid, gp,
    adj_p, out_p, adj_in, out_in, adj, c_send, c_sib, c_nbr,
    loc_sem, f_send, f_recv, w_send, w_recv, a_send, a_recv, c_sends, c_recvs,
):
    r, z = lax.axis_index("row"), lax.axis_index("rep")
    k = lax.rem(r, 2)
    sib = r + 1 - 2 * k
    mate = z + 1 - 2 * lax.rem(z, 2)
    bit2, bit4 = lax.rem(lax.div(r, 2), 2), lax.rem(lax.div(r, 4), 2)
    near, far = r + 2 - 4 * bit2, r + 4 - 8 * bit4
    rows, quarter = cot_ref.shape
    half = rows // 2
    row_blocks = rows // 128
    slots = vals_ref.shape[1]
    feat = w_in_ref.shape[0]
    hidw = w_in_ref.shape[1]
    has_up, has_dn = r + 2 < n_row, r >= 2
    peers = [lax.rem(z + i, n_rep) for i in range(1, n_rep)]
    froms = [lax.rem(z + n_rep - i, n_rep) for i in range(1, n_rep)]

    def remote(src, dst, send, recv, dev):
        return pltpu.make_async_remote_copy(
            src_ref=src, dst_ref=dst, send_sem=send, recv_sem=recv, device_id=dev, device_id_type=MESH
        )

    def panel(ref, slot):
        return ref.at[pl.ds(pl.multiple_of(slot * rows, rows), rows)]

    def halves(ref, s):
        return ref.at[pl.ds(pl.multiple_of(s * half, half), half)]

    barrier = pltpu.get_barrier_semaphore()
    for zp in peers:
        pl.semaphore_signal(barrier, inc=1, device_id=(r, zp), device_id_type=MESH)
    pl.semaphore_signal(barrier, inc=1, device_id=(sib, z), device_id_type=MESH)

    pl.semaphore_signal(barrier, inc=1, device_id=(far, z), device_id_type=MESH)

    @pl.when(has_up)
    def _():
        pl.semaphore_signal(barrier, inc=1, device_id=(r + 2, z), device_id_type=MESH)

    @pl.when(has_dn)
    def _():
        pl.semaphore_signal(barrier, inc=1, device_id=(r - 2, z), device_id_type=MESH)

    columns = pl.ds(pl.multiple_of(z * quarter, quarter), quarter)
    own_copy = pltpu.make_async_copy(feats_ref.at[:, columns], panel(ext, 2), loc_sem)
    own_copy.start()
    own_copy.wait()
    pl.semaphore_wait(barrier, n_rep + 1 + has_up.astype(jnp.int32) + has_dn.astype(jnp.int32))

    own = panel(ext, 2)
    f_up = remote(own, panel(ext, 0), f_send.at[0], f_recv.at[0], (r + 2, z))
    f_dn = remote(own, panel(ext, 4), f_send.at[1], f_recv.at[1], (r - 2, z))
    f_sib = remote(own, panel(ext, 1 + 2 * k), f_send.at[2], f_recv.at[2], (sib, z))
    f_fwd = remote(
        panel(ext, 4 - 4 * k), panel(ext, 3 - 2 * k), f_send.at[3], f_recv.at[3], (sib, z)
    )
    from_dn = remote(own, panel(ext, 0), f_send.at[0], f_recv.at[0], (r - 2, z))
    from_up = remote(own, panel(ext, 4), f_send.at[1], f_recv.at[1], (r + 2, z))
    from_sib = remote(own, panel(ext, 3 - 2 * k), f_send.at[2], f_recv.at[2], (sib, z))
    from_fwd = remote(own, panel(ext, 1 + 2 * k), f_send.at[3], f_recv.at[3], (sib, z))
    fwd_out = jnp.where(k == 0, r + 2 < n_row, r >= 2)
    fwd_in = jnp.where(k == 0, r >= 2, r + 2 < n_row)

    @pl.when(has_up)
    def _():
        f_up.start()

    @pl.when(has_dn)
    def _():
        f_dn.start()

    f_sib.start()
    cot_out = [
        remote(halves(cot_ref, lax.rem(zp, 2)), cot_full.at[z], a_send.at[0, i], a_recv.at[0, i], (r, zp))
        for i, zp in enumerate(peers)
    ]
    eighth = feat // 8
    quad, pair = 4 * k, 4 * k + 2 * bit2

    def span(ref, start, count):
        return ref.at[pl.ds(pl.multiple_of(start * eighth, eighth), count * eighth)]

    def round_of(step, start, count, dev, first=False):
        ends = ((w_in_ref if first else w2_in, w2_in), (w_out_ref if first else w2_out, w2_out))
        return [
            remote(
                span(src, start, count), span(dst, start, count),
                w_send.at[2 * step + i], w_recv.at[2 * step + i], dev,
            )
            for i, (src, dst) in enumerate(ends)
        ]

    w_rounds = [
        round_of(0, pair + bit4, 1, (r, mate), True),
        round_of(1, pair + bit4, 1, (far, z)),
        round_of(2, pair, 2, (near, z)),
        round_of(3, quad, 4, (sib, z)),
    ]
    w_lands = [
        w_rounds[0],
        round_of(1, pair + 1 - bit4, 1, (far, z)),
        round_of(2, quad + 2 - 2 * bit2, 2, (near, z)),
        round_of(3, 4 - quad, 4, (sib, z)),
    ]

    def pass_weights(step):
        if step:
            for copy in w_lands[step - 1]:
                copy.wait_recv()
        if step < 4:
            for copy in w_rounds[step]:
                copy.start()

    pass_weights(0)

    @pl.when(jnp.logical_not(has_dn))
    def _():
        ext[0:rows] = jnp.zeros((rows, quarter), BF16)

    @pl.when(jnp.logical_not(has_up))
    def _():
        ext[4 * rows : 5 * rows] = jnp.zeros((rows, quarter), BF16)

    @pl.when(r < 1)
    def _():
        ext[rows : 2 * rows] = jnp.zeros((rows, quarter), BF16)

    @pl.when(r + 1 >= n_row)
    def _():
        ext[3 * rows : 4 * rows] = jnp.zeros((rows, quarter), BF16)

    cot_full[z] = cot_ref[pl.ds(pl.multiple_of(lax.rem(z, 2) * half, half), half), :]

    def transpose_block(b, carry):
        for s in range(slots):
            vals_t[b, s] = vals_ref[b, s].astype(F32).T.astype(BF16)
        return carry

    lax.fori_loop(0, row_blocks, transpose_block, 0)

    def fill_dense(t, carry):
        at = pl.ds(pl.multiple_of(t * 128, 128), 128)
        for b in range(row_blocks):
            straight = jnp.zeros((8, 16, 128), BF16)
            turned = jnp.zeros((8, 16, 128), BF16)
            for s in range(slots):
                row = mask_ref[t, b * slots + s : b * slots + s + 1, :]
                keep = jnp.broadcast_to(row, (16, 128)).astype(BF16)[None]
                straight = straight + vals_ref[b, s].reshape(8, 16, 128) * keep
                turned = turned + vals_t[b, s].reshape(8, 16, 128) * keep
            dense[b * 128 : (b + 1) * 128, at] = straight.reshape(128, 128)
            dense_t[at, b * 128 : (b + 1) * 128] = turned.reshape(128, 128)
        return carry

    lax.fori_loop(0, 5 * row_blocks, fill_dense, 0)
    pass_weights(1)
    for copy in cot_out:
        copy.start()

    def gather(slot, first=False):
        inner = pl.ds(pl.multiple_of(slot * rows, rows), rows)

        def step(m, carry):
            at = pl.ds(pl.multiple_of(m * 256, 256), 256)
            part = dot(dense[at, inner], ext[inner, :])
            agg_acc[at, :] = part if first else agg_acc[at, :] + part
            return carry

        lax.fori_loop(0, rows // 256, step, 0)

    gather(2, True)
    from_sib.wait_recv()
    gather(3 - 2 * k)

    @pl.when(has_dn)
    def _():
        from_dn.wait_recv()

    @pl.when(has_up)
    def _():
        from_up.wait_recv()

    @pl.when(fwd_out)
    def _():
        f_fwd.start()

    pass_weights(2)
    gather(0)
    gather(4)

    @pl.when(fwd_in)
    def _():
        from_fwd.wait_recv()

    gather(1 + 2 * k)
    agg[...] = agg_acc[...].astype(BF16)
    agg_out = [
        remote(halves(agg, lax.rem(zp, 2)), agg_full.at[z], a_send.at[1, i], a_recv.at[1, i], (r, zp))
        for i, zp in enumerate(peers)
    ]
    for copy in agg_out:
        copy.start()
    agg_full[z] = agg[pl.ds(pl.multiple_of(lax.rem(z, 2) * half, half), half), :]

    def arrivals(buf, kind):
        return [
            remote(buf.at[zf], buf.at[zf], a_send.at[kind, i], a_recv.at[kind, i], (r, zf))
            for i, zf in enumerate(froms)
        ]

    pass_weights(3)
    for copy in arrivals(cot_full, 0) + arrivals(agg_full, 1):
        copy.wait_recv()

    tile = 256

    def hidden_part(w_a, w_b, base):
        def step(i, carry):
            hc = pl.ds(pl.multiple_of(i * tile, tile), tile)
            to = pl.ds(pl.multiple_of(base + i * tile, tile), tile)
            wa, wb = w_a[:, hc], w_b[:, hc]
            for m in range(half // tile):
                rs = slice(m * tile, (m + 1) * tile)
                x = jnp.concatenate([agg_full[q, rs] for q in range(n_rep)], axis=1)
                c = jnp.concatenate([cot_full[q, rs] for q in range(n_rep)], axis=1)
                value, slope = gelu_pair(dot(x, wa))
                hid[rs, to] = value.astype(BF16)
                gp[rs, to] = (dot(c, wb) * slope).astype(BF16)
            return carry

        lax.fori_loop(0, hidw // tile, step, 0)

    hidden_part(w_in_ref, w_out_ref, 0)
    pass_weights(4)
    hidden_part(w2_in, w2_out, hidw)

    def product(src, w_a, w_b, dst, zq):
        at = pl.ds(pl.multiple_of(zq * quarter, quarter), quarter)
        wa, wb = w_a[at, :], w_b[at, :]
        for m in range(half // tile):
            rs = slice(m * tile, (m + 1) * tile)
            res = dot(src[rs, :hidw], wa, ((1,), (1,))) + dot(src[rs, hidw:], wb, ((1,), (1,)))
            dst[zq, rs] = res.astype(BF16)

    def spread(src, w_a, w_b, part, landing, kind):
        sent = []
        for i, zp in enumerate(peers):
            product(src, w_a, w_b, part, zp)
            copy = remote(
                part.at[zp], landing.at[z], a_send.at[kind, i], a_recv.at[kind, i], (r, zp)
            )
            copy.start()
            sent.append(copy)
        product(src, w_a, w_b, part, z)
        landing[z] = part[z]
        return sent

    adj_out = spread(gp, w_in_ref, w2_in, adj_p, adj_in, 2)
    out_out = spread(hid, w_out_ref, w2_out, out_p, out_in, 3)

    for copy in arrivals(adj_in, 2):
        copy.wait_recv()
    for s in range(2):
        total = adj_in[s].astype(F32)
        for q in range(s + 2, n_rep, 2):
            total = total + adj_in[q].astype(F32)
        adj[s * half : (s + 1) * half] = total.astype(BF16)

    def piece(p, m):
        at = pl.ds(pl.multiple_of(p * rows + m * tile, tile), tile)
        return dot(dense_t[at, :], adj[...])

    def put(p, slot):
        def step(m, carry):
            at = pl.ds(pl.multiple_of(m * tile, tile), tile)
            c_send[slot, at, :] = piece(p, m).astype(BF16)
            return carry

        lax.fori_loop(0, rows // tile, step, 0)

    plain_to, helped_to = r - 2 + 4 * k, r + 2 - 4 * k
    c_help = remote(c_send.at[0], c_sib.at[0], c_sends.at[0], c_recvs.at[0], (sib, z))
    c_own = remote(c_send.at[1], c_sib.at[1], c_sends.at[1], c_recvs.at[1], (sib, z))
    c_plain = remote(
        c_send.at[2], c_nbr.at[1 - k], c_sends.at[2], c_recvs.at[3 - k], (plain_to, z)
    )
    c_helped = remote(
        c_send.at[3], c_nbr.at[k], c_sends.at[3], c_recvs.at[2 + k], (helped_to, z)
    )
    put(1 + 2 * k, 0)
    c_help.start()
    put(4 * k, 2)
    plain_ok, helped_ok = fwd_in, fwd_out

    @pl.when(plain_ok)
    def _():
        c_plain.start()

    c_help.wait_recv()

    def add_help(m, carry):
        at = pl.ds(pl.multiple_of(m * tile, tile), tile)
        total = piece(4 - 4 * k, m) + c_sib[0, at, :].astype(F32)
        c_send[3, at, :] = total.astype(BF16)
        return carry

    lax.fori_loop(0, rows // tile, add_help, 0)

    @pl.when(helped_ok)
    def _():
        c_helped.start()

    put(3 - 2 * k, 1)
    c_own.start()

    for copy in arrivals(out_in, 3):
        copy.wait_recv()
    for s in range(2):
        total = out_in[s].astype(F32)
        for q in range(s + 2, n_rep, 2):
            total = total + out_in[q].astype(F32)
        mine = ext[2 * rows + s * half : 2 * rows + (s + 1) * half]
        upd_ref[s * half : (s + 1) * half] = (mine.astype(F32) + total).astype(BF16)

    c_own.wait_recv()
    from_low = remote(c_nbr.at[0], c_nbr.at[0], c_sends.at[2], c_recvs.at[2], (r - 2, z))
    from_high = remote(c_nbr.at[1], c_nbr.at[1], c_sends.at[3], c_recvs.at[3], (r + 2, z))

    @pl.when(has_dn)
    def _():
        from_low.wait_recv()

    @pl.when(jnp.logical_not(has_dn))
    def _():
        c_nbr[0] = jnp.zeros((rows, quarter), BF16)

    @pl.when(has_up)
    def _():
        from_high.wait_recv()

    @pl.when(jnp.logical_not(has_up))
    def _():
        c_nbr[1] = jnp.zeros((rows, quarter), BF16)

    def finish(m, carry):
        at = pl.ds(pl.multiple_of(m * tile, tile), tile)
        total = piece(2, m) + c_sib[1, at, :].astype(F32)
        total = total + c_nbr[0, at, :].astype(F32) + c_nbr[1, at, :].astype(F32)
        grad_ref[at, :] = (cot_ref[at, :].astype(F32) + total).astype(BF16)
        return carry

    lax.fori_loop(0, rows // tile, finish, 0)

    for copy in cot_out + sum(w_rounds, []) + agg_out + adj_out + out_out + [f_sib, c_help, c_own]:
        copy.wait_send()
    for ok, copy in (
        (has_up, f_up), (has_dn, f_dn), (fwd_out, f_fwd), (plain_ok, c_plain), (helped_ok, c_helped)
    ):
        pl.when(ok)(copy.wait_send)


def body(n_row, n_rep, node_feats, block_cols, block_vals, w_in, w_out, cotangent):
    rows, quarter = cotangent.shape
    feat = node_feats.shape[1]
    row_blocks, slots = block_cols.shape
    hidw = w_in.shape[1]
    half = rows // 2
    first = (lax.axis_index("row") - 2) * row_blocks
    position = jnp.where(block_cols >= 0, block_cols - first, -1).reshape(1, -1, 1)
    landing = jnp.arange(5 * row_blocks, dtype=jnp.int32).reshape(-1, 1, 1)
    mask = jnp.broadcast_to(
        (position == landing).astype(F32), (5 * row_blocks, row_blocks * slots, 128)
    )
    vmem = pl.BlockSpec(memory_space=pltpu.VMEM)
    dma = pltpu.SemaphoreType.DMA
    return pl.pallas_call(
        functools.partial(kernel, n_row, n_rep),
        out_shape=(jax.ShapeDtypeStruct((rows, quarter), BF16),) * 2,
        in_specs=[vmem, pl.BlockSpec(memory_space=pl.ANY), vmem, vmem, vmem, vmem],
        out_specs=(vmem, vmem),
        scratch_shapes=[
            pltpu.VMEM((5 * rows, quarter), BF16),
            pltpu.VMEM((row_blocks, slots, 128, 128), BF16),
            pltpu.VMEM((rows, 5 * rows), BF16),
            pltpu.VMEM((5 * rows, rows), BF16),
            pltpu.VMEM((rows, quarter), F32),
            pltpu.VMEM((feat, hidw), BF16),
            pltpu.VMEM((feat, hidw), BF16),
            pltpu.VMEM((n_rep, half, quarter), BF16),
            pltpu.VMEM((rows, quarter), BF16),
            pltpu.VMEM((n_rep, half, quarter), BF16),
            pltpu.VMEM((half, 2 * hidw), BF16),
            pltpu.VMEM((half, 2 * hidw), BF16),
            pltpu.VMEM((n_rep, half, quarter), BF16),
            pltpu.VMEM((n_rep, half, quarter), BF16),
            pltpu.VMEM((n_rep, half, quarter), BF16),
            pltpu.VMEM((n_rep, half, quarter), BF16),
            pltpu.VMEM((rows, quarter), BF16),
            pltpu.VMEM((4, rows, quarter), BF16),
            pltpu.VMEM((2, rows, quarter), BF16),
            pltpu.VMEM((2, rows, quarter), BF16),
            dma,
            dma((4,)),
            dma((4,)),
            dma((8,)),
            dma((8,)),
            dma((4, n_rep - 1)),
            dma((4, n_rep - 1)),
            dma((4,)),
            dma((4,)),
        ],
        compiler_params=pltpu.CompilerParams(
            collective_id=0, has_side_effects=True, vmem_limit_bytes=60 * 1024 * 1024
        ),
    )(mask, node_feats, block_vals, w_in, w_out, cotangent)


def solution(mesh):
    in_specs = (
        P("row", None),
        P("row", None),
        P("row", None, None, None),
        P(None, "rep"),
        P(None, "rep"),
        P("row", "rep"),
    )
    out_specs = (P("row", "rep"), P("row", "rep"))
    run = functools.partial(body, mesh.shape["row"], mesh.shape["rep"])
    return jax.shard_map(run, mesh=mesh, in_specs=in_specs, out_specs=out_specs, check_vma=False)
```

profile of v0, /device:TPU:28, one launch (start us, length us, event | category | flops | bytes accessed | tf_op | source)
XLA Modules:
  0.0 146.3 jit_solution(9515999087649081946)
XLA Ops:
  0.6 0.7 subtract_select_fusion
  1.3 0.1 copy.9
  1.4 0.1 eq.20
  1.5 1.1 broadcast_in_dim.10.mask_ref
  2.6 140.0 %shard_map.77 = (bf16[1024,256]{1,0:T(8,128)(2,1)}, bf16[1024,256]{1,0:T(8,128)(2,1)}) custom-call(f32[40,32,128]{2,1,0:T(8,128)} %broadcast_in_dim.10.mask_ref, bf16[1024,1024]{1,0:T(8,128)(2,1)} %feats_ref.1, bf16[8,4,128,128]{3,2,1,0:T(8,128)(2,1)} %vals_ref.1, bf16[1024,1024]{1,0:T(8,128)(2,1)} %w_in_ref.1, bf16[1024,1024]{1,0:T(8,128)(2,1)} %w_out_ref.1, ...), custom_call_target="tpu_custom_call" | custom-call | tf_op jit(solution)/shard_map/pallas_call | solution.py:410
  142.6 1.9 %copy.12 = bf16[1024,256]{1,0:T(8,128)(2,1)} copy(bf16[1024,256]{1,0:T(8,128)(2,1)} %get-tuple-element.4) | data formatting | bytes 1048576
  144.4 1.9 %copy.13 = bf16[1024,256]{1,0:T(8,128)(2,1)} copy(bf16[1024,256]{1,0:T(8,128)(2,1)} %get-tuple-element.5) | data formatting | bytes 1048576
  (1 shorter events, 0.0 us)
where the time goes:
time: 147 us; the launch traced here: 146 us
  Pallas kernels  140 us (95%)
  local copies, waits for them, and re-layouts  4.99 us (3%)
    pallas_call x1, Pallas kernels, body(): pl.pallas_call(functools.partial(kernel, n_row, n_rep), out_shape=(jax.Sh...  140 us
    unnamed x2, local copies, waits for them, and re-layouts  3.74 us

commit v1 on v0

v1 whole, which is shorter than its diff:
```python
import functools

import jax
import jax.numpy as jnp
from jax import lax
from jax.experimental import pallas as pl
from jax.experimental.pallas import tpu as pltpu
from jax.sharding import PartitionSpec as P

F32 = jnp.float32
BF16 = jnp.bfloat16
MESH = pl.DeviceIdType.MESH
PARTS = 2


def dot(a, b, dims=((1,), (0,))):
    return lax.dot_general(a, b, (dims, ((), ())), preferred_element_type=F32)


def gelu_pair(v):
    c = 0.7978845608
    vv = v * v
    t = jnp.tanh(c * (v + 0.044715 * v * vv))
    half = 0.5 * (1.0 + t)
    value = v * half
    slope = half + 0.5 * v * (1.0 - t * t) * c * (1.0 + 3.0 * 0.044715 * vv)
    return value, slope


def kernel(
    n_row, n_rep, cols_ref, spread_ref, feats_ref, vals_ref, w_in_ref, w_out_ref, cot_ref,
    upd_ref, grad_ref,
    ext, marks, vals, vals_t, dense_t, w1_in, w1_out, w2_in, w2_out, cot, cot_full, agg, agg_full, hid, gp,
    adj_p, out_p, adj_in, out_in, adj, c_send, c_sib, c_nbr,
    loc_sem, f_send, f_recv, w_send, w_recv, a_send, a_recv, c_sends, c_recvs,
):
    r, z = lax.axis_index("row"), lax.axis_index("rep")
    k = lax.rem(r, 2)
    sib = r + 1 - 2 * k
    z1, z2 = lax.rem(z, 2), lax.div(z, 2)
    mate = z + 1 - 2 * z1
    peers = [z + 2 - 4 * z2, n_rep - 1 - z, mate]
    bit2, bit4 = lax.rem(lax.div(r, 2), 2), lax.rem(lax.div(r, 4), 2)
    near, far = r + 2 - 4 * bit2, r + 4 - 8 * bit4
    rows, quarter = cot.shape
    half = rows // 2
    part = half // PARTS
    row_blocks, slots = cols_ref.shape
    feat, hidw = w1_in.shape
    has_up, has_dn = r + 2 < n_row, r >= 2
    first = (r - 2) * row_blocks

    def remote(src, dst, send, recv, dev):
        return pltpu.make_async_remote_copy(
            src_ref=src, dst_ref=dst, send_sem=send, recv_sem=recv, device_id=dev, device_id_type=MESH
        )

    def panel(ref, slot):
        return ref.at[pl.ds(slot * row_blocks, row_blocks)]

    def half_part(ref, s, c, count=1):
        start = pl.multiple_of(s * half + c * part, part)
        return ref.at[pl.ds(start, count * part)]

    barrier = pltpu.get_barrier_semaphore()
    for zp in peers:
        pl.semaphore_signal(barrier, inc=1, device_id=(r, zp), device_id_type=MESH)
    pl.semaphore_signal(barrier, inc=1, device_id=(sib, z), device_id_type=MESH)
    pl.semaphore_signal(barrier, inc=1, device_id=(far, z), device_id_type=MESH)

    @pl.when(has_up)
    def _():
        pl.semaphore_signal(barrier, inc=1, device_id=(r + 2, z), device_id_type=MESH)

    @pl.when(has_dn)
    def _():
        pl.semaphore_signal(barrier, inc=1, device_id=(r - 2, z), device_id_type=MESH)

    columns = pl.ds(pl.multiple_of(z * quarter, quarter), quarter)
    own_copy = pltpu.make_async_copy(feats_ref.at[:, :, columns], panel(ext, 2), loc_sem.at[0])
    loads = [
        pltpu.make_async_copy(src, dst, loc_sem.at[1 + i])
        for i, (src, dst) in enumerate(
            (
                (vals_ref, vals),
                (half_part(cot_ref, z1, 0, PARTS), cot_full.at[z]),
                (w_in_ref, w1_in),
                (w_out_ref, w1_out),
                (cot_ref, cot),
            )
        )
    ]
    own_copy.start()
    for copy in loads:
        copy.start()
    own_copy.wait()
    pl.semaphore_wait(barrier, n_rep + 1 + has_up.astype(jnp.int32) + has_dn.astype(jnp.int32))

    own = panel(ext, 2)
    f_up = remote(own, panel(ext, 0), f_send.at[0], f_recv.at[0], (r + 2, z))
    f_dn = remote(own, panel(ext, 4), f_send.at[1], f_recv.at[1], (r - 2, z))
    f_sib = remote(own, panel(ext, 1 + 2 * k), f_send.at[2], f_recv.at[2], (sib, z))
    f_fwd = remote(
        panel(ext, 4 - 4 * k), panel(ext, 3 - 2 * k), f_send.at[3], f_recv.at[3], (sib, z)
    )
    from_dn = remote(own, panel(ext, 0), f_send.at[0], f_recv.at[0], (r - 2, z))
    from_up = remote(own, panel(ext, 4), f_send.at[1], f_recv.at[1], (r + 2, z))
    from_sib = remote(own, panel(ext, 3 - 2 * k), f_send.at[2], f_recv.at[2], (sib, z))
    from_fwd = remote(own, panel(ext, 1 + 2 * k), f_send.at[3], f_recv.at[3], (sib, z))
    fwd_out = jnp.where(k == 0, r + 2 < n_row, r >= 2)
    fwd_in = jnp.where(k == 0, r >= 2, r + 2 < n_row)

    @pl.when(has_up)
    def _():
        f_up.start()

    @pl.when(has_dn)
    def _():
        f_dn.start()

    f_sib.start()

    eighth = feat // 8

    def span(ref, start, count):
        return ref.at[pl.ds(pl.multiple_of(start * eighth, eighth), count * eighth)]

    def rounds(raw, full, base, bit_a, dev_a, bit_b, dev_b):
        mine = 4 * k + 2 * bit_b + bit_a
        plan = (
            (raw, mine, mine, 1, (r, mate)),
            (full, mine, mine + 1 - 2 * bit_a, 1, (dev_a, z)),
            (full, 4 * k + 2 * bit_b, 4 * k + 2 - 2 * bit_b, 2, (dev_b, z)),
            (full, 4 * k, 4 - 4 * k, 4, (sib, z)),
        )
        sent, got = [], []
        for i, (src, lo, there, count, dev) in enumerate(plan):
            sems = (w_send.at[base + i], w_recv.at[base + i])
            sent.append(remote(span(src, lo, count), span(full, lo, count), *sems, dev))
            got.append(remote(span(full, there, count), span(full, there, count), *sems, dev))
        return sent, got

    in_sent, in_got = rounds(w_in_ref, w2_in, 0, bit2, near, bit4, far)
    out_sent, out_got = rounds(w_out_ref, w2_out, 4, bit4, far, bit2, near)

    def exchange(src, dst, kind, c, count=1):
        return [
            remote(
                half_part(src, lax.rem(zp, 2), c, count),
                dst.at[z, pl.ds(c * part, count * part)],
                a_send.at[kind, i], a_recv.at[kind, i], (r, zp),
            )
            for i, zp in enumerate(peers)
        ]

    def arrivals(buf, kind, c, count=1):
        views = [buf.at[zf, pl.ds(c * part, count * part)] for zf in peers]
        return [
            remote(v, v, a_send.at[kind, i], a_recv.at[kind, i], (r, zf))
            for i, (v, zf) in enumerate(zip(views, peers))
        ]

    in_sent[0].start()
    out_sent[0].start()
    cot_out = exchange(cot_ref, cot_full, 0, 0, PARTS)
    for copy in cot_out:
        copy.start()

    @pl.when(jnp.logical_not(has_dn))
    def _():
        ext[0:row_blocks] = jnp.zeros((row_blocks, 128, quarter), BF16)

    @pl.when(jnp.logical_not(has_up))
    def _():
        ext[4 * row_blocks : 5 * row_blocks] = jnp.zeros((row_blocks, 128, quarter), BF16)

    @pl.when(r < 1)
    def _():
        ext[row_blocks : 2 * row_blocks] = jnp.zeros((row_blocks, 128, quarter), BF16)

    @pl.when(r + 1 >= n_row)
    def _():
        ext[3 * row_blocks : 4 * row_blocks] = jnp.zeros((row_blocks, 128, quarter), BF16)

    for copy in loads:
        copy.wait()

    def transpose_block(b, carry):
        for s in range(slots):
            vals_t[b, s] = vals[b, s].astype(F32).T.astype(BF16)
        return carry

    lax.fori_loop(0, row_blocks, transpose_block, 0)

    for b in range(row_blocks):
        for s in range(slots):
            col = jnp.broadcast_to(spread_ref[b : b + 1, s : s + 1], (16, 128))
            marks[b * slots + s] = jnp.where(col >= 0, col - first, -1)

    def fill_dense(t, carry):
        at = pl.ds(pl.multiple_of(t * 128, 128), 128)
        for b in range(row_blocks):
            turned = jnp.zeros((8, 16, 128), BF16)
            for s in range(slots):
                keep = jnp.where(marks[b * slots + s] == t, 1.0, 0.0).astype(BF16)[None]
                turned = turned + vals_t[b, s].reshape(8, 16, 128) * keep
            dense_t[at, b * 128 : (b + 1) * 128] = turned.reshape(128, 128)
        return carry

    out_got[0].wait_recv()
    out_sent[1].start()
    in_got[0].wait_recv()

    @pl.when(has_dn)
    def _():
        from_dn.wait_recv()

    @pl.when(has_up)
    def _():
        from_up.wait_recv()

    @pl.when(fwd_out)
    def _():
        f_fwd.start()

    in_sent[1].start()
    from_sib.wait_recv()

    @pl.when(fwd_in)
    def _():
        from_fwd.wait_recv()

    def gather(b):
        left, right = [], []
        for s in range(slots):
            col = cols_ref[b, s]
            absent = lax.shift_right_logical(col, 31)
            place = col - first + absent * (1 + first + 2 * row_blocks + b)
            keep = jnp.where(marks[b * slots + s] >= 0, 1.0, 0.0).astype(BF16)[None]
            left.append((vals[b, s].reshape(8, 16, 128) * keep).reshape(128, 128))
            right.append(ext[jnp.minimum(jnp.maximum(place, 0), 5 * row_blocks - 1)])
        res = dot(jnp.concatenate(left, axis=1), jnp.concatenate(right, axis=0))
        agg[b * 128 : (b + 1) * 128, :] = res.astype(BF16)

    agg_out = []
    per_part = part // 128
    for c in range(PARTS):
        for s in range(2):
            for i in range(per_part):
                gather((s * PARTS + c) * per_part + i)
        sent = exchange(agg, agg_full, 1 + c, c)
        for copy in sent:
            copy.start()
        agg_out += sent
    for c in range(PARTS):
        agg_full[z, pl.ds(c * part, part)] = agg[
            pl.ds(pl.multiple_of(z1 * half + c * part, part), part), :
        ]

    cut = 3 * row_blocks
    lax.fori_loop(0, cut, fill_dense, 0)
    in_got[1].wait_recv()
    in_sent[2].start()
    out_got[1].wait_recv()
    out_sent[2].start()
    lax.fori_loop(cut, 5 * row_blocks, fill_dense, 0)
    tile = 256

    def hidden_part(w_a, w_b, base, c):
        rs = pl.ds(c * part, part)

        def step(i, carry):
            hc = pl.ds(pl.multiple_of(i * tile, tile), tile)
            to = pl.ds(pl.multiple_of(base + i * tile, tile), tile)
            x = jnp.concatenate([agg_full[q, rs] for q in range(n_rep)], axis=1)
            g = jnp.concatenate([cot_full[q, rs] for q in range(n_rep)], axis=1)
            value, slope = gelu_pair(dot(x, w_a[:, hc]))
            hid[rs, to] = value.astype(BF16)
            gp[rs, to] = (dot(g, w_b[:, hc]) * slope).astype(BF16)
            return carry

        lax.fori_loop(0, hidw // tile, step, 0)

    def product(src, w_a, w_b, dst, zq, c):
        at = pl.ds(pl.multiple_of(zq * quarter, quarter), quarter)
        rs = pl.ds(c * part, part)
        res = dot(src[rs, :hidw], w_a[at, :], ((1,), (1,)))
        res = res + dot(src[rs, hidw:], w_b[at, :], ((1,), (1,)))
        dst[zq, rs] = res.astype(BF16)

    def spread(src, w_a, w_b, made, landing, kind, c):
        sent = []
        for i, zp in enumerate(peers):
            product(src, w_a, w_b, made, zp, c)
            rs = pl.ds(c * part, part)
            copy = remote(
                made.at[zp, rs], landing.at[z, rs], a_send.at[kind, i], a_recv.at[kind, i], (r, zp)
            )
            copy.start()
            sent.append(copy)
        product(src, w_a, w_b, landing, z, c)
        return sent

    for copy in arrivals(cot_full, 0, 0, PARTS):
        copy.wait_recv()
    adj_out, out_out = [], []
    for c in range(PARTS):
        for copy in arrivals(agg_full, 1 + c, c):
            copy.wait_recv()
        hidden_part(w1_in, w1_out, 0, c)
        if c == 0:
            in_got[2].wait_recv()
            in_sent[3].start()
            out_got[2].wait_recv()
            out_sent[3].start()
            in_got[3].wait_recv()
            out_got[3].wait_recv()
        hidden_part(w2_in, w2_out, hidw, c)
        adj_out += spread(gp, w1_in, w2_in, adj_p, adj_in, 1 + PARTS + c, c)
    for c in range(PARTS):
        out_out += spread(hid, w1_out, w2_out, out_p, out_in, 1 + 2 * PARTS + c, c)

    for c in range(PARTS):
        for copy in arrivals(adj_in, 1 + PARTS + c, c):
            copy.wait_recv()
    for s in range(2):
        total = adj_in[s].astype(F32)
        for q in range(s + 2, n_rep, 2):
            total = total + adj_in[q].astype(F32)
        adj[s * half : (s + 1) * half] = total.astype(BF16)

    def piece(p, m):
        at = pl.ds(pl.multiple_of(p * rows + m * tile, tile), tile)
        return dot(dense_t[at, :], adj[...])

    def put(p, slot):
        def step(m, carry):
            at = pl.ds(pl.multiple_of(m * tile, tile), tile)
            c_send[slot, at, :] = piece(p, m).astype(BF16)
            return carry

        lax.fori_loop(0, rows // tile, step, 0)

    plain_to, helped_to = r - 2 + 4 * k, r + 2 - 4 * k
    c_help = remote(c_send.at[0], c_sib.at[0], c_sends.at[0], c_recvs.at[0], (sib, z))
    c_own = remote(c_send.at[1], c_sib.at[1], c_sends.at[1], c_recvs.at[1], (sib, z))
    c_plain = remote(
        c_send.at[2], c_nbr.at[1 - k], c_sends.at[2], c_recvs.at[3 - k], (plain_to, z)
    )
    c_helped = remote(
        c_send.at[3], c_nbr.at[k], c_sends.at[3], c_recvs.at[2 + k], (helped_to, z)
    )
    put(1 + 2 * k, 0)
    c_help.start()
    put(4 * k, 2)
    plain_ok, helped_ok = fwd_in, fwd_out

    @pl.when(plain_ok)
    def _():
        c_plain.start()

    c_help.wait_recv()

    def add_help(m, carry):
        at = pl.ds(pl.multiple_of(m * tile, tile), tile)
        total = piece(4 - 4 * k, m) + c_sib[0, at, :].astype(F32)
        c_send[3, at, :] = total.astype(BF16)
        return carry

    lax.fori_loop(0, rows // tile, add_help, 0)

    @pl.when(helped_ok)
    def _():
        c_helped.start()

    put(3 - 2 * k, 1)
    c_own.start()

    for c in range(PARTS):
        for copy in arrivals(out_in, 1 + 2 * PARTS + c, c):
            copy.wait_recv()
    for s in range(2):
        total = out_in[s].astype(F32)
        for q in range(s + 2, n_rep, 2):
            total = total + out_in[q].astype(F32)
        start, count = 2 * row_blocks + s * row_blocks // 2, row_blocks // 2
        mine = ext[start : start + count].reshape(half, quarter)
        upd_ref[s * half : (s + 1) * half] = (mine.astype(F32) + total).astype(BF16)

    c_own.wait_recv()
    from_low = remote(c_nbr.at[0], c_nbr.at[0], c_sends.at[2], c_recvs.at[2], (r - 2, z))
    from_high = remote(c_nbr.at[1], c_nbr.at[1], c_sends.at[3], c_recvs.at[3], (r + 2, z))

    @pl.when(has_dn)
    def _():
        from_low.wait_recv()

    @pl.when(jnp.logical_not(has_dn))
    def _():
        c_nbr[0] = jnp.zeros((rows, quarter), BF16)

    @pl.when(has_up)
    def _():
        from_high.wait_recv()

    @pl.when(jnp.logical_not(has_up))
    def _():
        c_nbr[1] = jnp.zeros((rows, quarter), BF16)

    def finish(m, carry):
        at = pl.ds(pl.multiple_of(m * tile, tile), tile)
        total = piece(2, m) + c_sib[1, at, :].astype(F32)
        total = total + c_nbr[0, at, :].astype(F32) + c_nbr[1, at, :].astype(F32)
        grad_ref[at, :] = (cot[at, :].astype(F32) + total).astype(BF16)
        return carry

    lax.fori_loop(0, rows // tile, finish, 0)

    for copy in cot_out + in_sent + out_sent + agg_out + adj_out + out_out + [f_sib, c_help, c_own]:
        copy.wait_send()
    for ok, copy in (
        (has_up, f_up), (has_dn, f_dn), (fwd_out, f_fwd), (plain_ok, c_plain), (helped_ok, c_helped)
    ):
        pl.when(ok)(copy.wait_send)


def body(n_row, n_rep, node_feats, block_cols, block_vals, w_in, w_out, cotangent):
    rows, quarter = cotangent.shape
    row_blocks, slots = block_cols.shape
    feat, hidw = w_in.shape
    half = rows // 2
    kinds = 1 + 3 * PARTS
    vmem = pl.BlockSpec(memory_space=pltpu.VMEM)
    anywhere = pl.BlockSpec(memory_space=pl.ANY)
    dma = pltpu.SemaphoreType.DMA
    return pl.pallas_call(
        functools.partial(kernel, n_row, n_rep),
        out_shape=(jax.ShapeDtypeStruct((rows, quarter), BF16),) * 2,
        in_specs=[pl.BlockSpec(memory_space=pltpu.SMEM), vmem] + [anywhere] * 5,
        out_specs=(vmem, vmem),
        scratch_shapes=[
            pltpu.VMEM((5 * row_blocks, 128, quarter), BF16),
            pltpu.VMEM((row_blocks * slots, 16, 128), jnp.int32),
            pltpu.VMEM((row_blocks, slots, 128, 128), BF16),
            pltpu.VMEM((row_blocks, slots, 128, 128), BF16),
            pltpu.VMEM((5 * rows, rows), BF16),
            pltpu.VMEM((feat, hidw), BF16),
            pltpu.VMEM((feat, hidw), BF16),
            pltpu.VMEM((feat, hidw), BF16),
            pltpu.VMEM((feat, hidw), BF16),
            pltpu.VMEM((rows, quarter), BF16),
            pltpu.VMEM((n_rep, half, quarter), BF16),
            pltpu.VMEM((rows, quarter), BF16),
            pltpu.VMEM((n_rep, half, quarter), BF16),
            pltpu.VMEM((half, 2 * hidw), BF16),
            pltpu.VMEM((half, 2 * hidw), BF16),
            pltpu.VMEM((n_rep, half, quarter), BF16),
            pltpu.VMEM((n_rep, half, quarter), BF16),
            pltpu.VMEM((n_rep, half, quarter), BF16),
            pltpu.VMEM((n_rep, half, quarter), BF16),
            pltpu.VMEM((rows, quarter), BF16),
            pltpu.VMEM((4, rows, quarter), BF16),
            pltpu.VMEM((2, rows, quarter), BF16),
            pltpu.VMEM((2, rows, quarter), BF16),
            dma((6,)),
            dma((4,)),
            dma((4,)),
            dma((8,)),
            dma((8,)),
            dma((kinds, n_rep - 1)),
            dma((kinds, n_rep - 1)),
            dma((4,)),
            dma((4,)),
        ],
        compiler_params=pltpu.CompilerParams(
            collective_id=0, has_side_effects=True, vmem_limit_bytes=60 * 1024 * 1024
        ),
    )(block_cols, block_cols, node_feats.reshape(row_blocks, 128, feat), block_vals, w_in, w_out, cotangent)


def solution(mesh):
    in_specs = (
        P("row", None),
        P("row", None),
        P("row", None, None, None),
        P(None, "rep"),
        P(None, "rep"),
        P("row", "rep"),
    )
    out_specs = (P("row", "rep"), P("row", "rep"))
    run = functools.partial(body, mesh.shape["row"], mesh.shape["rep"])
    return jax.shard_map(run, mesh=mesh, in_specs=in_specs, out_specs=out_specs, check_vma=False)
```

time: 147 us -> 124 us (0.84)
  the two profiles are of different devices: /device:TPU:28 before, /device:TPU:19 now
where the time goes in v1:
time: 124 us
  Pallas kernels  118 us (95%)
  local copies, waits for them, and re-layouts  5.08 us (4%)
    pallas_call x1, Pallas kernels, body(): pl.pallas_call(functools.partial(kernel, n_row, n_rep), out_shape=(jax.Sh...  118 us
    unnamed x3, local copies, waits for them, and re-layouts  5.08 us

profile of v1, /device:TPU:19, one launch (start us, length us, event | category | flops | bytes accessed | tf_op | source)
XLA Modules:
  0.0 123.8 jit_solution(3448097485053055309)
XLA Ops:
  0.6 1.3 %copy.8.cols_ref.spread_ref = s32[8,4]{1,0:T(8,128)} copy(s32[8,4]{0,1:T(4,128)} %param.7) | data formatting | bytes 256 | tf_op args[1]
  2.0 118.1 %shard_map.77 = (bf16[1024,256]{1,0:T(8,128)(2,1)}, bf16[1024,256]{1,0:T(8,128)(2,1)}) custom-call(s32[8,4]{1,0:T(8,128)} %copy.8.cols_ref.spread_ref, s32[8,4]{1,0:T(8,128)} %copy.8.cols_ref.spread_ref, bf16[8,128,1024]{2,1,0:T(8,128)(2,1)} %bitcast.1, bf16[8,4,128,128]{3,2,1,0:T(8,128)(2,1)} %vals_ref.1, bf16[1024,1024]{1,0:T(8,128)(2,1)} %w_in_ref.1, ...), custom_call_target="tpu_custom_call" | custom-call | tf_op jit(solution)/shard_map/pallas_call | solution.py:436
  120.1 1.9 %copy.12 = bf16[1024,256]{1,0:T(8,128)(2,1)} copy(bf16[1024,256]{1,0:T(8,128)(2,1)} %get-tuple-element.4) | data formatting | bytes 1048576
  122.0 1.9 %copy.13 = bf16[1024,256]{1,0:T(8,128)(2,1)} copy(bf16[1024,256]{1,0:T(8,128)(2,1)} %get-tuple-element.5) | data formatting | bytes 1048576

commit v2 on v1

--- a/solution.py
+++ b/solution.py
@@ -11,6 +11,7 @@
 BF16 = jnp.bfloat16
 MESH = pl.DeviceIdType.MESH
 PARTS = 2
+WIDE = 2
 
 
 def dot(a, b, dims=((1,), (0,))):
@@ -45,6 +46,7 @@
     rows, quarter = cot.shape
     half = rows // 2
     part = half // PARTS
+    width = quarter // WIDE
     row_blocks, slots = cols_ref.shape
     feat, hidw = w1_in.shape
     has_up, has_dn = r + 2 < n_row, r >= 2
@@ -248,10 +250,10 @@
         for s in range(2):
             for i in range(per_part):
                 gather((s * PARTS + c) * per_part + i)
-        sent = exchange(agg, agg_full, 1 + c, c)
-        for copy in sent:
-            copy.start()
-        agg_out += sent
+        agg_out.append(exchange(agg, agg_full, 1 + c, c))
+        if c == 0:
+            for copy in agg_out[0]:
+                copy.start()
     for c in range(PARTS):
         agg_full[z, pl.ds(c * part, part)] = agg[
             pl.ds(pl.multiple_of(z1 * half + c * part, part), part), :
@@ -263,6 +265,11 @@
     in_sent[2].start()
     out_got[1].wait_recv()
     out_sent[2].start()
+    for c in range(1, PARTS):
+        for copy in agg_out[c - 1]:
+            copy.wait_send()
+        for copy in agg_out[c]:
+            copy.start()
     lax.fori_loop(cut, 5 * row_blocks, fill_dense, 0)
     tile = 256
 
@@ -281,29 +288,35 @@
 
         lax.fori_loop(0, hidw // tile, step, 0)
 
-    def product(src, w_a, w_b, dst, zq, c):
+    def product(src, w_a, w_b, zq, c):
         at = pl.ds(pl.multiple_of(zq * quarter, quarter), quarter)
         rs = pl.ds(c * part, part)
         res = dot(src[rs, :hidw], w_a[at, :], ((1,), (1,)))
         res = res + dot(src[rs, hidw:], w_b[at, :], ((1,), (1,)))
-        dst[zq, rs] = res.astype(BF16)
-
-    def spread(src, w_a, w_b, made, landing, kind, c):
-        sent = []
-        for i, zp in enumerate(peers):
-            product(src, w_a, w_b, made, zp, c)
-            rs = pl.ds(c * part, part)
-            copy = remote(
-                made.at[zp, rs], landing.at[z, rs], a_send.at[kind, i], a_recv.at[kind, i], (r, zp)
+        return res.astype(BF16)
+
+    def adj_copies(f, c):
+        kind = 1 + PARTS + f * PARTS + c
+        rs = pl.ds(c * part, part)
+        return [
+            remote(
+                adj_p.at[zp, f, rs], adj_in.at[z, f, rs],
+                a_send.at[kind, i], a_recv.at[kind, i], (r, zp),
             )
-            copy.start()
-            sent.append(copy)
-        product(src, w_a, w_b, landing, z, c)
-        return sent
+            for i, zp in enumerate(peers)
+        ]
+
+    def adj_arrivals(f, c):
+        kind = 1 + PARTS + f * PARTS + c
+        views = [adj_in.at[zf, f, pl.ds(c * part, part)] for zf in peers]
+        return [
+            remote(v, v, a_send.at[kind, i], a_recv.at[kind, i], (r, zf))
+            for i, (v, zf) in enumerate(zip(views, peers))
+        ]
 
     for copy in arrivals(cot_full, 0, 0, PARTS):
         copy.wait_recv()
-    adj_out, out_out = [], []
+    adj_sent = [[adj_copies(f, c) for c in range(PARTS)] for f in range(WIDE)]
     for c in range(PARTS):
         for copy in arrivals(agg_full, 1 + c, c):
             copy.wait_recv()
@@ -316,68 +329,140 @@
             in_got[3].wait_recv()
             out_got[3].wait_recv()
         hidden_part(w2_in, w2_out, hidw, c)
-        adj_out += spread(gp, w1_in, w2_in, adj_p, adj_in, 1 + PARTS + c, c)
+        rs = pl.ds(c * part, part)
+        for i, zp in enumerate(peers + [z]):
+            res = product(gp, w1_in, w2_in, zp, c)
+            made = adj_p if i < n_rep - 1 else adj_in
+            for f in range(WIDE):
+                made[zp, f, rs] = res[:, f * width : (f + 1) * width]
+            if i < n_rep - 1:
+                adj_sent[0][c][i].start()
+
+    out_sends = []
     for c in range(PARTS):
-        out_out += spread(hid, w1_out, w2_out, out_p, out_in, 1 + 2 * PARTS + c, c)
-
-    for c in range(PARTS):
-        for copy in arrivals(adj_in, 1 + PARTS + c, c):
-            copy.wait_recv()
-    for s in range(2):
-        total = adj_in[s].astype(F32)
-        for q in range(s + 2, n_rep, 2):
-            total = total + adj_in[q].astype(F32)
-        adj[s * half : (s + 1) * half] = total.astype(BF16)
-
-    def piece(p, m):
+        rs = pl.ds(c * part, part)
+        kind = 1 + (1 + WIDE) * PARTS + c
+        for i, zp in enumerate(peers):
+            out_p[zp, rs] = product(hid, w1_out, w2_out, zp, c)
+            out_sends.append(
+                remote(
+                    out_p.at[zp, rs], out_in.at[z, rs],
+                    a_send.at[kind, i], a_recv.at[kind, i], (r, zp),
+                )
+            )
+        out_in[z, rs] = product(hid, w1_out, w2_out, z, c)
+
+    tile = 256
+    plain_to, helped_to = r - 2 + 4 * k, r + 2 - 4 * k
+    plain_ok, helped_ok = fwd_in, fwd_out
+    p5_sent = []
+
+    def turn(f):
+        for c in range(PARTS):
+            for copy in adj_arrivals(f, c):
+                copy.wait_recv()
+        for s in range(2):
+            total = adj_in[s, f].astype(F32)
+            for q in range(s + 2, n_rep, 2):
+                total = total + adj_in[q, f].astype(F32)
+            adj[f, s * half : (s + 1) * half] = total.astype(BF16)
+
+        def put(p, slot):
+            def step(m, carry):
+                at = pl.ds(pl.multiple_of(m * tile, tile), tile)
+                c_send[4 * f + slot, at, :] = piece(f, p, m).astype(BF16)
+                return carry
+
+            lax.fori_loop(0, rows // tile, step, 0)
+
+        def cross(slot, dst, got, dev):
+            return remote(
+                c_send.at[4 * f + slot], dst, c_sends.at[4 * f + slot], c_recvs.at[4 * f + got], dev
+            )
+
+        c_help = cross(0, c_sib.at[2 * f], 0, (sib, z))
+        c_own = cross(1, c_sib.at[2 * f + 1], 1, (sib, z))
+        c_plain = cross(2, c_nbr.at[2 * f + 1 - k], 3 - k, (plain_to, z))
+        c_helped = cross(3, c_nbr.at[2 * f + k], 2 + k, (helped_to, z))
+        put(1 + 2 * k, 0)
+        c_help.start()
+        put(4 * k, 2)
+
+        @pl.when(plain_ok)
+        def _():
+            c_plain.start()
+
+        c_help.wait_recv()
+
+        def add_help(m, carry):
+            at = pl.ds(pl.multiple_of(m * tile, tile), tile)
+            total = piece(f, 4 - 4 * k, m) + c_sib[2 * f, at, :].astype(F32)
+            c_send[4 * f + 3, at, :] = total.astype(BF16)
+            return carry
+
+        lax.fori_loop(0, rows // tile, add_help, 0)
+
+        @pl.when(helped_ok)
+        def _():
+            c_helped.start()
+
+        put(3 - 2 * k, 1)
+        c_own.start()
+        p5_sent.append((c_help, c_own, c_plain, c_helped))
+
+    def piece(f, p, m):
         at = pl.ds(pl.multiple_of(p * rows + m * tile, tile), tile)
-        return dot(dense_t[at, :], adj[...])
-
-    def put(p, slot):
+        return dot(dense_t[at, :], adj[f])
+
+    def finish(f):
+        p5_sent[f][1].wait_recv()
+        from_low = remote(
+            c_nbr.at[2 * f], c_nbr.at[2 * f], c_sends.at[4 * f + 2], c_recvs.at[4 * f + 2], (r - 2, z)
+        )
+        from_high = remote(
+            c_nbr.at[2 * f + 1], c_nbr.at[2 * f + 1], c_sends.at[4 * f + 3], c_recvs.at[4 * f + 3],
+            (r + 2, z),
+        )
+
+        @pl.when(has_dn)
+        def _():
+            from_low.wait_recv()
+
+        @pl.when(jnp.logical_not(has_dn))
+        def _():
+            c_nbr[2 * f] = jnp.zeros((rows, width), BF16)
+
+        @pl.when(has_up)
+        def _():
+            from_high.wait_recv()
+
+        @pl.when(jnp.logical_not(has_up))
+        def _():
+            c_nbr[2 * f + 1] = jnp.zeros((rows, width), BF16)
+
+        cs = slice(f * width, (f + 1) * width)
+
         def step(m, carry):
             at = pl.ds(pl.multiple_of(m * tile, tile), tile)
-            c_send[slot, at, :] = piece(p, m).astype(BF16)
+            total = piece(f, 2, m) + c_sib[2 * f + 1, at, :].astype(F32)
+            total = total + c_nbr[2 * f, at, :].astype(F32) + c_nbr[2 * f + 1, at, :].astype(F32)
+            grad_ref[at, cs] = (cot[at, cs].astype(F32) + total).astype(BF16)
             return carry
 
         lax.fori_loop(0, rows // tile, step, 0)
 
-    plain_to, helped_to = r - 2 + 4 * k, r + 2 - 4 * k
-    c_help = remote(c_send.at[0], c_sib.at[0], c_sends.at[0], c_recvs.at[0], (sib, z))
-    c_own = remote(c_send.at[1], c_sib.at[1], c_sends.at[1], c_recvs.at[1], (sib, z))
-    c_plain = remote(
-        c_send.at[2], c_nbr.at[1 - k], c_sends.at[2], c_recvs.at[3 - k], (plain_to, z)
-    )
-    c_helped = remote(
-        c_send.at[3], c_nbr.at[k], c_sends.at[3], c_recvs.at[2 + k], (helped_to, z)
-    )
-    put(1 + 2 * k, 0)
-    c_help.start()
-    put(4 * k, 2)
-    plain_ok, helped_ok = fwd_in, fwd_out
-
-    @pl.when(plain_ok)
-    def _():
-        c_plain.start()
-
-    c_help.wait_recv()
-
-    def add_help(m, carry):
-        at = pl.ds(pl.multiple_of(m * tile, tile), tile)
-        total = piece(4 - 4 * k, m) + c_sib[0, at, :].astype(F32)
-        c_send[3, at, :] = total.astype(BF16)
-        return carry
-
-    lax.fori_loop(0, rows // tile, add_help, 0)
-
-    @pl.when(helped_ok)
-    def _():
-        c_helped.start()
-
-    put(3 - 2 * k, 1)
-    c_own.start()
-
+    for f in range(WIDE):
+        for copies in adj_sent[f]:
+            for copy in copies:
+                copy.wait_send()
+        following = sum(adj_sent[f + 1], []) if f + 1 < WIDE else out_sends
+        for copy in following:
+            copy.start()
+        turn(f)
+    for f in range(WIDE - 1):
+        finish(f)
     for c in range(PARTS):
-        for copy in arrivals(out_in, 1 + 2 * PARTS + c, c):
+        for copy in arrivals(out_in, 1 + (1 + WIDE) * PARTS + c, c):
             copy.wait_recv()
     for s in range(2):
         total = out_in[s].astype(F32)
@@ -386,41 +471,16 @@
         start, count = 2 * row_blocks + s * row_blocks // 2, row_blocks // 2
         mine = ext[start : start + count].reshape(half, quarter)
         upd_ref[s * half : (s + 1) * half] = (mine.astype(F32) + total).astype(BF16)
-
-    c_own.wait_recv()
-    from_low = remote(c_nbr.at[0], c_nbr.at[0], c_sends.at[2], c_recvs.at[2], (r - 2, z))
-    from_high = remote(c_nbr.at[1], c_nbr.at[1], c_sends.at[3], c_recvs.at[3], (r + 2, z))
-
-    @pl.when(has_dn)
-    def _():
-        from_low.wait_recv()
-
-    @pl.when(jnp.logical_not(has_dn))
-    def _():
-        c_nbr[0] = jnp.zeros((rows, quarter), BF16)
-
-    @pl.when(has_up)
-    def _():
-        from_high.wait_recv()
-
-    @pl.when(jnp.logical_not(has_up))
-    def _():
-        c_nbr[1] = jnp.zeros((rows, quarter), BF16)
-
-    def finish(m, carry):
-        at = pl.ds(pl.multiple_of(m * tile, tile), tile)
-        total = piece(2, m) + c_sib[1, at, :].astype(F32)
-        total = total + c_nbr[0, at, :].astype(F32) + c_nbr[1, at, :].astype(F32)
-        grad_ref[at, :] = (cot[at, :].astype(F32) + total).astype(BF16)
-        return carry
-
-    lax.fori_loop(0, rows // tile, finish, 0)
-
-    for copy in cot_out + in_sent + out_sent + agg_out + adj_out + out_out + [f_sib, c_help, c_own]:
+    finish(WIDE - 1)
+
+    for copy in cot_out + in_sent + out_sent + agg_out[-1] + out_sends + [f_sib]:
         copy.wait_send()
-    for ok, copy in (
-        (has_up, f_up), (has_dn, f_dn), (fwd_out, f_fwd), (plain_ok, c_plain), (helped_ok, c_helped)
-    ):
+    late = [(has_up, f_up), (has_dn, f_dn), (fwd_out, f_fwd)]
+    for c_help, c_own, c_plain, c_helped in p5_sent:
+        c_help.wait_send()
+        c_own.wait_send()
+        late += [(plain_ok, c_plain), (helped_ok, c_helped)]
+    for ok, copy in late:
         pl.when(ok)(copy.wait_send)
 
 
@@ -429,7 +489,8 @@
     row_blocks, slots = block_cols.shape
     feat, hidw = w_in.shape
     half = rows // 2
-    kinds = 1 + 3 * PARTS
+    kinds = 1 + (2 + WIDE) * PARTS
+    width = quarter // WIDE
     vmem = pl.BlockSpec(memory_space=pltpu.VMEM)
     anywhere = pl.BlockSpec(memory_space=pl.ANY)
     dma = pltpu.SemaphoreType.DMA
@@ -454,14 +515,14 @@
             pltpu.VMEM((n_rep, half, quarter), BF16),
             pltpu.VMEM((half, 2 * hidw), BF16),
             pltpu.VMEM((half, 2 * hidw), BF16),
+            pltpu.VMEM((n_rep, WIDE, half, width), BF16),
             pltpu.VMEM((n_rep, half, quarter), BF16),
+            pltpu.VMEM((n_rep, WIDE, half, width), BF16),
             pltpu.VMEM((n_rep, half, quarter), BF16),
-            pltpu.VMEM((n_rep, half, quarter), BF16),
-            pltpu.VMEM((n_rep, half, quarter), BF16),
-            pltpu.VMEM((rows, quarter), BF16),
-            pltpu.VMEM((4, rows, quarter), BF16),
-            pltpu.VMEM((2, rows, quarter), BF16),
-            pltpu.VMEM((2, rows, quarter), BF16),
+            pltpu.VMEM((WIDE, rows, width), BF16),
+            pltpu.VMEM((4 * WIDE, rows, width), BF16),
+            pltpu.VMEM((2 * WIDE, rows, width), BF16),
+            pltpu.VMEM((2 * WIDE, rows, width), BF16),
             dma((6,)),
             dma((4,)),
             dma((4,)),
@@ -469,8 +530,8 @@
             dma((8,)),
             dma((kinds, n_rep - 1)),
             dma((kinds, n_rep - 1)),
-            dma((4,)),
-            dma((4,)),
+            dma((4 * WIDE,)),
+            dma((4 * WIDE,)),
         ],
         compiler_params=pltpu.CompilerParams(
             collective_id=0, has_side_effects=True, vmem_limit_bytes=60 * 1024 * 1024

time: 124 us -> 116 us (0.935)
  Pallas kernels: 118 us -> 110 us
    pallas_call x1, Pallas kernels: 118 us -> 110 us  [body(): pl.pallas_call(functools.partial(kernel, n_row, n_rep), out_shape=(jax.Sh...]
where the time goes in v2:
time: 116 us; the launch traced here: 115 us
  Pallas kernels  110 us (95%)
  local copies, waits for them, and re-layouts  5.08 us (4%)
    pallas_call x1, Pallas kernels, body(): pl.pallas_call(functools.partial(kernel, n_row, n_rep), out_shape=(jax.Sh...  110 us
    unnamed x3, local copies, waits for them, and re-layouts  5.08 us

profile of v2, /device:TPU:19, one launch (start us, length us, event | category | flops | bytes accessed | tf_op | source)
XLA Modules:
  0.0 115.3 jit_solution(7201627325183148863)
XLA Ops:
  0.6 1.3 %copy.8.cols_ref.spread_ref = s32[8,4]{1,0:T(8,128)} copy(s32[8,4]{0,1:T(4,128)} %param.7) | data formatting | bytes 256 | tf_op args[1]
  2.0 109.6 %shard_map.77 = (bf16[1024,256]{1,0:T(8,128)(2,1)}, bf16[1024,256]{1,0:T(8,128)(2,1)}) custom-call(s32[8,4]{1,0:T(8,128)} %copy.8.cols_ref.spread_ref, s32[8,4]{1,0:T(8,128)} %copy.8.cols_ref.spread_ref, bf16[8,128,1024]{2,1,0:T(8,128)(2,1)} %bitcast.1, bf16[8,4,128,128]{3,2,1,0:T(8,128)(2,1)} %vals_ref.1, bf16[1024,1024]{1,0:T(8,128)(2,1)} %w_in_ref.1, ...), custom_call_target="tpu_custom_call" | custom-call | tf_op jit(solution)/shard_map/pallas_call | solution.py:497
  111.6 1.9 %copy.12 = bf16[1024,256]{1,0:T(8,128)(2,1)} copy(bf16[1024,256]{1,0:T(8,128)(2,1)} %get-tuple-element.4) | data formatting | bytes 1048576
  113.5 1.9 %copy.13 = bf16[1024,256]{1,0:T(8,128)(2,1)} copy(bf16[1024,256]{1,0:T(8,128)(2,1)} %get-tuple-element.5) | data formatting | bytes 1048576

commit v3 on v2

--- a/solution.py
+++ b/solution.py
@@ -12,6 +12,7 @@
 MESH = pl.DeviceIdType.MESH
 PARTS = 2
 WIDE = 2
+CUTS = 4
 
 
 def dot(a, b, dims=((1,), (0,))):
@@ -30,8 +31,8 @@
 
 def kernel(
     n_row, n_rep, cols_ref, spread_ref, feats_ref, vals_ref, w_in_ref, w_out_ref, cot_ref,
-    upd_ref, grad_ref,
-    ext, marks, vals, vals_t, dense_t, w1_in, w1_out, w2_in, w2_out, cot, cot_full, agg, agg_full, hid, gp,
+    upd_hbm, grad_hbm,
+    upd_ref, grad_ref, ext, marks, vals, vals_t, dense_t, w1_in, w1_out, w2_in, w2_out, cot, cot_full, agg, agg_full, hid, gp,
     adj_p, out_p, adj_in, out_in, adj, c_send, c_sib, c_nbr,
     loc_sem, f_send, f_recv, w_send, w_recv, a_send, a_recv, c_sends, c_recvs,
 ):
@@ -47,7 +48,7 @@
     half = rows // 2
     part = half // PARTS
     width = quarter // WIDE
-    row_blocks, slots = cols_ref.shape
+    slots, row_blocks = cols_ref.shape
     feat, hidw = w1_in.shape
     has_up, has_dn = r + 2 < n_row, r >= 2
     first = (r - 2) * row_blocks
@@ -196,7 +197,7 @@
 
     for b in range(row_blocks):
         for s in range(slots):
-            col = jnp.broadcast_to(spread_ref[b : b + 1, s : s + 1], (16, 128))
+            col = jnp.broadcast_to(spread_ref[s : s + 1, b : b + 1], (16, 128))
             marks[b * slots + s] = jnp.where(col >= 0, col - first, -1)
 
     def fill_dense(t, carry):
@@ -235,7 +236,7 @@
     def gather(b):
         left, right = [], []
         for s in range(slots):
-            col = cols_ref[b, s]
+            col = cols_ref[s, b]
             absent = lax.shift_right_logical(col, 31)
             place = col - first + absent * (1 + first + 2 * row_blocks + b)
             keep = jnp.where(marks[b * slots + s] >= 0, 1.0, 0.0).astype(BF16)[None]
@@ -459,20 +460,25 @@
         for copy in following:
             copy.start()
         turn(f)
-    for f in range(WIDE - 1):
+    for f in range(WIDE):
         finish(f)
+    grad_out = pltpu.make_async_copy(grad_ref, grad_hbm, loc_sem.at[6])
+    grad_out.start()
     for c in range(PARTS):
         for copy in arrivals(out_in, 1 + (1 + WIDE) * PARTS + c, c):
             copy.wait_recv()
-    for s in range(2):
-        total = out_in[s].astype(F32)
-        for q in range(s + 2, n_rep, 2):
-            total = total + out_in[q].astype(F32)
-        start, count = 2 * row_blocks + s * row_blocks // 2, row_blocks // 2
-        mine = ext[start : start + count].reshape(half, quarter)
-        upd_ref[s * half : (s + 1) * half] = (mine.astype(F32) + total).astype(BF16)
-    finish(WIDE - 1)
-
+        rs = pl.ds(c * part, part)
+        for s in range(2):
+            total = out_in[s, rs].astype(F32)
+            for q in range(s + 2, n_rep, 2):
+                total = total + out_in[q, rs].astype(F32)
+            start, count = 2 * row_blocks + s * row_blocks // 2 + c * per_part, per_part
+            mine = ext[start : start + count].reshape(part, quarter)
+            at = pl.ds(s * half + c * part, part)
+            upd_ref[at] = (mine.astype(F32) + total).astype(BF16)
+
+    upd_out = pltpu.make_async_copy(upd_ref, upd_hbm, loc_sem.at[7])
+    upd_out.start()
     for copy in cot_out + in_sent + out_sent + agg_out[-1] + out_sends + [f_sib]:
         copy.wait_send()
     late = [(has_up, f_up), (has_dn, f_dn), (fwd_out, f_fwd)]
@@ -482,6 +488,27 @@
         late += [(plain_ok, c_plain), (helped_ok, c_helped)]
     for ok, copy in late:
         pl.when(ok)(copy.wait_send)
+    grad_out.wait()
+    upd_out.wait()
+
+
+def settle(upd_ref, grad_ref, upd_out, grad_out, held, sems):
+    size = upd_ref.shape[0] // CUTS
+    steps = []
+    for i in range(CUTS):
+        rs = pl.ds(i * size, size)
+        for j, (src, dst) in enumerate(((upd_ref, upd_out), (grad_ref, grad_out))):
+            steps.append((
+                pltpu.make_async_copy(src.at[rs], held.at[j, rs], sems.at[0, j, i]),
+                pltpu.make_async_copy(held.at[j, rs], dst.at[rs], sems.at[1, j, i]),
+            ))
+    for load, _ in steps:
+        load.start()
+    for load, store in steps:
+        load.wait()
+        store.start()
+    for _, store in steps:
+        store.wait()
 
 
 def body(n_row, n_rep, node_feats, block_cols, block_vals, w_in, w_out, cotangent):
@@ -494,12 +521,14 @@
     vmem = pl.BlockSpec(memory_space=pltpu.VMEM)
     anywhere = pl.BlockSpec(memory_space=pl.ANY)
     dma = pltpu.SemaphoreType.DMA
-    return pl.pallas_call(
+    made = pl.pallas_call(
         functools.partial(kernel, n_row, n_rep),
         out_shape=(jax.ShapeDtypeStruct((rows, quarter), BF16),) * 2,
         in_specs=[pl.BlockSpec(memory_space=pltpu.SMEM), vmem] + [anywhere] * 5,
-        out_specs=(vmem, vmem),
+        out_specs=(anywhere, anywhere),
         scratch_shapes=[
+            pltpu.VMEM((rows, quarter), BF16),
+            pltpu.VMEM((rows, quarter), BF16),
             pltpu.VMEM((5 * row_blocks, 128, quarter), BF16),
             pltpu.VMEM((row_blocks * slots, 16, 128), jnp.int32),
             pltpu.VMEM((row_blocks, slots, 128, 128), BF16),
@@ -523,7 +552,7 @@
             pltpu.VMEM((4 * WIDE, rows, width), BF16),
             pltpu.VMEM((2 * WIDE, rows, width), BF16),
             pltpu.VMEM((2 * WIDE, rows, width), BF16),
-            dma((6,)),
+            dma((8,)),
             dma((4,)),
             dma((4,)),
             dma((8,)),
@@ -536,7 +565,14 @@
         compiler_params=pltpu.CompilerParams(
             collective_id=0, has_side_effects=True, vmem_limit_bytes=60 * 1024 * 1024
         ),
-    )(block_cols, block_cols, node_feats.reshape(row_blocks, 128, feat), block_vals, w_in, w_out, cotangent)
+    )(block_cols.T, block_cols.T, node_feats.reshape(row_blocks, 128, feat), block_vals, w_in, w_out, cotangent)
+    return pl.pallas_call(
+        settle,
+        out_shape=(jax.ShapeDtypeStruct((rows, quarter), BF16),) * 2,
+        in_specs=[anywhere] * 2,
+        out_specs=(anywhere,) * 2,
+        scratch_shapes=[pltpu.VMEM((2, rows, quarter), BF16), dma((2, 2, CUTS))],
+    )(*made)
 
 
 def solution(mesh):

time: 116 us -> 112 us (0.966)
  local copies, waits for them, and re-layouts: 5.08 us -> 0 us
    unnamed x3 -> x0, local copies, waits for them, and re-layouts: 5.08 us -> none
    pallas_call x0 -> x1, Pallas kernels: none -> 2.09 us  [body(): pl.pallas_call(settle, out_shape=(jax.ShapeDtypeStruct((rows, quarter), B...]
where the time goes in v3:
time: 112 us
  Pallas kernels  111 us (99%)
    pallas_call x1, Pallas kernels, body(): pl.pallas_call(functools.partial(kernel, n_row, n_rep), out_shape=(jax.Sh...  109 us

profile of v3, /device:TPU:19, one launch (start us, length us, event | category | flops | bytes accessed | tf_op | source)
XLA Modules:
  0.0 112.1 jit_solution(3341003479396643738)
XLA Ops:
  0.6 109.3 %shard_map.77 = (bf16[1024,256]{1,0:T(8,128)(2,1)}, bf16[1024,256]{1,0:T(8,128)(2,1)}) custom-call(s32[4,8]{1,0:T(4,128)} %bitcast.3, s32[4,8]{1,0:T(4,128)} %bitcast.4, bf16[8,128,1024]{2,1,0:T(8,128)(2,1)} %bitcast.2, bf16[8,4,128,128]{3,2,1,0:T(8,128)(2,1)} %vals_ref.1, bf16[1024,1024]{1,0:T(8,128)(2,1)} %w_in_ref.1, bf16[1024,1024]{1,0:T(8,128)(2,1)} %w_out_ref.1, ...), custom_call_target="tpu_custom_call" | custom-call | tf_op jit(solution)/shard_map/pallas_call | solution.py:524
  110.0 2.1 %shard_map.78 = (bf16[1024,256]{1,0:T(8,128)(2,1)}, bf16[1024,256]{1,0:T(8,128)(2,1)}) custom-call(bf16[1024,256]{1,0:T(8,128)(2,1)} %get-tuple-element.4.upd_ref, bf16[1024,256]{1,0:T(8,128)(2,1)} %get-tuple-element.5.grad_ref), custom_call_target="tpu_custom_call" | custom-call | tf_op jit(solution)/shard_map/pallas_call | solution.py:569

commit v4 on v3

--- a/solution.py
+++ b/solution.py
@@ -33,8 +33,8 @@
     n_row, n_rep, cols_ref, spread_ref, feats_ref, vals_ref, w_in_ref, w_out_ref, cot_ref,
     upd_hbm, grad_hbm,
     upd_ref, grad_ref, ext, marks, vals, vals_t, dense_t, w1_in, w1_out, w2_in, w2_out, cot, cot_full, agg, agg_full, hid, gp,
-    adj_p, out_p, adj_in, out_in, adj, c_send, c_sib, c_nbr,
-    loc_sem, f_send, f_recv, w_send, w_recv, a_send, a_recv, c_sends, c_recvs,
+    adj_p, out_p, adj_in, out_in, adj, c_send, c_sib, c_nbr, f_relay, c_relay,
+    loc_sem, f_send, f_recv, w_send, w_recv, a_send, a_recv, c_sends, c_recvs, b_sends, b_recvs,
 ):
     r, z = lax.axis_index("row"), lax.axis_index("rep")
     k = lax.rem(r, 2)
@@ -51,6 +51,11 @@
     slots, row_blocks = cols_ref.shape
     feat, hidw = w1_in.shape
     has_up, has_dn = r + 2 < n_row, r >= 2
+    turning, passing = bit2 != bit4, bit2 == bit4
+    turn_up, turn_dn = jnp.logical_and(turning, bit2 == 1), jnp.logical_and(turning, bit2 == 0)
+    straight_up = jnp.logical_and(has_up, jnp.logical_not(turn_up))
+    straight_dn = jnp.logical_and(has_dn, jnp.logical_not(turn_dn))
+    hb = row_blocks // 2
     first = (r - 2) * row_blocks
 
     def remote(src, dst, send, recv, dev):
@@ -100,27 +105,38 @@
     pl.semaphore_wait(barrier, n_rep + 1 + has_up.astype(jnp.int32) + has_dn.astype(jnp.int32))
 
     own = panel(ext, 2)
-    f_up = remote(own, panel(ext, 0), f_send.at[0], f_recv.at[0], (r + 2, z))
-    f_dn = remote(own, panel(ext, 4), f_send.at[1], f_recv.at[1], (r - 2, z))
+
+    def some(slot, h):
+        return ext.at[pl.ds(slot * row_blocks + h * hb, hb)]
+
+    f_up = remote(some(2, 0), some(0, 0), f_send.at[0], f_recv.at[0], (r + 2, z))
+    f_dn = remote(some(2, 0), some(4, 0), f_send.at[1], f_recv.at[1], (r - 2, z))
+    f_up2 = remote(some(2, 1), some(0, 1), f_send.at[4], f_recv.at[4], (r + 2, z))
+    f_dn2 = remote(some(2, 1), some(4, 1), f_send.at[5], f_recv.at[5], (r - 2, z))
+    f_out = remote(some(2, 1), f_relay, f_send.at[6], f_recv.at[6], (far, z))
+    f_on = remote(f_relay, some(4 - 4 * bit2, 1), f_send.at[7], f_recv.at[5 - bit2], (near, z))
     f_sib = remote(own, panel(ext, 1 + 2 * k), f_send.at[2], f_recv.at[2], (sib, z))
     f_fwd = remote(
         panel(ext, 4 - 4 * k), panel(ext, 3 - 2 * k), f_send.at[3], f_recv.at[3], (sib, z)
     )
-    from_dn = remote(own, panel(ext, 0), f_send.at[0], f_recv.at[0], (r - 2, z))
-    from_up = remote(own, panel(ext, 4), f_send.at[1], f_recv.at[1], (r + 2, z))
+    from_dn = [
+        remote(some(0, h), some(0, h), f_send.at[4 * h], f_recv.at[4 * h], (r - 2, z))
+        for h in range(2)
+    ]
+    from_up = [
+        remote(some(4, h), some(4, h), f_send.at[4 * h + 1], f_recv.at[4 * h + 1], (r + 2, z))
+        for h in range(2)
+    ]
     from_sib = remote(own, panel(ext, 3 - 2 * k), f_send.at[2], f_recv.at[2], (sib, z))
     from_fwd = remote(own, panel(ext, 1 + 2 * k), f_send.at[3], f_recv.at[3], (sib, z))
     fwd_out = jnp.where(k == 0, r + 2 < n_row, r >= 2)
     fwd_in = jnp.where(k == 0, r >= 2, r + 2 < n_row)
 
-    @pl.when(has_up)
-    def _():
-        f_up.start()
-
-    @pl.when(has_dn)
-    def _():
-        f_dn.start()
-
+    starts = (
+        (turning, f_out), (has_up, f_up), (has_dn, f_dn), (straight_up, f_up2), (straight_dn, f_dn2)
+    )
+    for ok, copy in starts:
+        pl.when(ok)(copy.start)
     f_sib.start()
 
     eighth = feat // 8
@@ -210,23 +226,25 @@
             dense_t[at, b * 128 : (b + 1) * 128] = turned.reshape(128, 128)
         return carry
 
-    out_got[0].wait_recv()
-    out_sent[1].start()
-    in_got[0].wait_recv()
+    @pl.when(passing)
+    def _():
+        f_out.wait_recv()
+        f_on.start()
 
     @pl.when(has_dn)
     def _():
-        from_dn.wait_recv()
+        for copy in from_dn:
+            copy.wait_recv()
 
     @pl.when(has_up)
     def _():
-        from_up.wait_recv()
+        for copy in from_up:
+            copy.wait_recv()
 
     @pl.when(fwd_out)
     def _():
         f_fwd.start()
 
-    in_sent[1].start()
     from_sib.wait_recv()
 
     @pl.when(fwd_in)
@@ -260,6 +278,10 @@
             pl.ds(pl.multiple_of(z1 * half + c * part, part), part), :
         ]
 
+    out_got[0].wait_recv()
+    out_sent[1].start()
+    in_got[0].wait_recv()
+    in_sent[1].start()
     cut = 3 * row_blocks
     lax.fori_loop(0, cut, fill_dense, 0)
     in_got[1].wait_recv()
@@ -356,6 +378,8 @@
     tile = 256
     plain_to, helped_to = r - 2 + 4 * k, r + 2 - 4 * k
     plain_ok, helped_ok = fwd_in, fwd_out
+    turn_plain = jnp.logical_and(turning, k == bit2)
+    turn_helped = jnp.logical_and(turning, k != bit2)
     p5_sent = []
 
     def turn(f):
@@ -383,16 +407,43 @@
 
         c_help = cross(0, c_sib.at[2 * f], 0, (sib, z))
         c_own = cross(1, c_sib.at[2 * f + 1], 1, (sib, z))
-        c_plain = cross(2, c_nbr.at[2 * f + 1 - k], 3 - k, (plain_to, z))
-        c_helped = cross(3, c_nbr.at[2 * f + k], 2 + k, (helped_to, z))
+        top, low = pl.ds(0, rows // 2), pl.ds(rows // 2, rows // 2)
+
+        def sides(slot, nbr, dev):
+            return (
+                remote(
+                    c_send.at[4 * f + slot, top], c_nbr.at[2 * f + nbr, top],
+                    c_sends.at[4 * f + slot], c_recvs.at[4 * f + 2 + nbr], dev,
+                ),
+                remote(
+                    c_send.at[4 * f + slot, low], c_nbr.at[2 * f + nbr, low],
+                    b_sends.at[4 * f + slot], b_recvs.at[4 * f + 2 + nbr], dev,
+                ),
+            )
+
+        c_plain = sides(2, 1 - k, (plain_to, z))
+        c_helped = sides(3, k, (helped_to, z))
+        c_out = remote(
+            c_send.at[4 * f + jnp.where(k == bit2, 2, 3), low], c_relay.at[f],
+            b_sends.at[4 * f], b_recvs.at[4 * f], (far, z),
+        )
+        c_on = remote(
+            c_relay.at[f], c_nbr.at[2 * f + 1 - bit2, low],
+            b_sends.at[4 * f + 1], b_recvs.at[4 * f + 3 - bit2], (near, z),
+        )
+        moves = (
+            (plain_ok, c_plain[0]), (jnp.logical_and(plain_ok, jnp.logical_not(turn_plain)), c_plain[1]),
+            (helped_ok, c_helped[0]),
+            (jnp.logical_and(helped_ok, jnp.logical_not(turn_helped)), c_helped[1]),
+            (turning, c_out), (passing, c_on),
+        )
         put(1 + 2 * k, 0)
         c_help.start()
         put(4 * k, 2)
 
-        @pl.when(plain_ok)
-        def _():
-            c_plain.start()
-
+        pl.when(turn_plain)(c_out.start)
+        for ok, copy in moves[:2]:
+            pl.when(ok)(copy.start)
         c_help.wait_recv()
 
         def add_help(m, carry):
@@ -403,13 +454,18 @@
 
         lax.fori_loop(0, rows // tile, add_help, 0)
 
-        @pl.when(helped_ok)
-        def _():
-            c_helped.start()
-
+        pl.when(turn_helped)(c_out.start)
+        for ok, copy in moves[2:4]:
+            pl.when(ok)(copy.start)
         put(3 - 2 * k, 1)
         c_own.start()
-        p5_sent.append((c_help, c_own, c_plain, c_helped))
+
+        @pl.when(passing)
+        def _():
+            c_out.wait_recv()
+            c_on.start()
+
+        p5_sent.append((c_help, c_own, moves))
 
     def piece(f, p, m):
         at = pl.ds(pl.multiple_of(p * rows + m * tile, tile), tile)
@@ -417,17 +473,15 @@
 
     def finish(f):
         p5_sent[f][1].wait_recv()
-        from_low = remote(
-            c_nbr.at[2 * f], c_nbr.at[2 * f], c_sends.at[4 * f + 2], c_recvs.at[4 * f + 2], (r - 2, z)
-        )
-        from_high = remote(
-            c_nbr.at[2 * f + 1], c_nbr.at[2 * f + 1], c_sends.at[4 * f + 3], c_recvs.at[4 * f + 3],
-            (r + 2, z),
-        )
+
+        def landed(nbr, dev):
+            for h, sems in enumerate((c_recvs, b_recvs)):
+                ref = c_nbr.at[2 * f + nbr, pl.ds(h * (rows // 2), rows // 2)]
+                remote(ref, ref, c_sends.at[4 * f + 2], sems.at[4 * f + 2 + nbr], (dev, z)).wait_recv()
 
         @pl.when(has_dn)
         def _():
-            from_low.wait_recv()
+            landed(0, r - 2)
 
         @pl.when(jnp.logical_not(has_dn))
         def _():
@@ -435,7 +489,7 @@
 
         @pl.when(has_up)
         def _():
-            from_high.wait_recv()
+            landed(1, r + 2)
 
         @pl.when(jnp.logical_not(has_up))
         def _():
@@ -481,11 +535,11 @@
     upd_out.start()
     for copy in cot_out + in_sent + out_sent + agg_out[-1] + out_sends + [f_sib]:
         copy.wait_send()
-    late = [(has_up, f_up), (has_dn, f_dn), (fwd_out, f_fwd)]
-    for c_help, c_own, c_plain, c_helped in p5_sent:
+    late = list(starts) + [(fwd_out, f_fwd), (passing, f_on)]
+    for c_help, c_own, moves in p5_sent:
         c_help.wait_send()
         c_own.wait_send()
-        late += [(plain_ok, c_plain), (helped_ok, c_helped)]
+        late += list(moves)
     for ok, copy in late:
         pl.when(ok)(copy.wait_send)
     grad_out.wait()
@@ -552,13 +606,17 @@
             pltpu.VMEM((4 * WIDE, rows, width), BF16),
             pltpu.VMEM((2 * WIDE, rows, width), BF16),
             pltpu.VMEM((2 * WIDE, rows, width), BF16),
+            pltpu.VMEM((row_blocks // 2, 128, quarter), BF16),
+            pltpu.VMEM((WIDE, rows // 2, width), BF16),
             dma((8,)),
-            dma((4,)),
-            dma((4,)),
+            dma((8,)),
+            dma((8,)),
             dma((8,)),
             dma((8,)),
             dma((kinds, n_rep - 1)),
             dma((kinds, n_rep - 1)),
+            dma((4 * WIDE,)),
+            dma((4 * WIDE,)),
             dma((4 * WIDE,)),
             dma((4 * WIDE,)),
         ],

time: 112 us -> 110 us (0.982); the launches traced: 112 us -> 109 us
  Pallas kernels: 111 us -> 108 us
    pallas_call x1, Pallas kernels: 109 us -> 106 us  [body(): pl.pallas_call(functools.partial(kernel, n_row, n_rep), out_shape=(jax.Sh...]
where the time goes in v4:
time: 110 us; the launch traced here: 109 us
  Pallas kernels  108 us (98%)
    pallas_call x1, Pallas kernels, body(): pl.pallas_call(functools.partial(kernel, n_row, n_rep), out_shape=(jax.Sh...  106 us

profile of v4, /device:TPU:19, one launch (start us, length us, event | category | flops | bytes accessed | tf_op | source)
XLA Modules:
  0.0 108.8 jit_solution(222747976337790987)
XLA Ops:
  0.6 106.0 %shard_map.77 = (bf16[1024,256]{1,0:T(8,128)(2,1)}, bf16[1024,256]{1,0:T(8,128)(2,1)}) custom-call(s32[4,8]{1,0:T(4,128)} %bitcast.3, s32[4,8]{1,0:T(4,128)} %bitcast.4, bf16[8,128,1024]{2,1,0:T(8,128)(2,1)} %bitcast.2, bf16[8,4,128,128]{3,2,1,0:T(8,128)(2,1)} %vals_ref.1, bf16[1024,1024]{1,0:T(8,128)(2,1)} %w_in_ref.1, bf16[1024,1024]{1,0:T(8,128)(2,1)} %w_out_ref.1, ...), custom_call_target="tpu_custom_call" | custom-call | tf_op jit(solution)/shard_map/pallas_call | solution.py:578
  106.7 2.1 %shard_map.78 = (bf16[1024,256]{1,0:T(8,128)(2,1)}, bf16[1024,256]{1,0:T(8,128)(2,1)}) custom-call(bf16[1024,256]{1,0:T(8,128)(2,1)} %get-tuple-element.4.upd_ref, bf16[1024,256]{1,0:T(8,128)(2,1)} %get-tuple-element.5.grad_ref), custom_call_target="tpu_custom_call" | custom-call | tf_op jit(solution)/shard_map/pallas_call | solution.py:627

commit v5 on v4

--- a/solution.py
+++ b/solution.py
@@ -270,9 +270,8 @@
             for i in range(per_part):
                 gather((s * PARTS + c) * per_part + i)
         agg_out.append(exchange(agg, agg_full, 1 + c, c))
-        if c == 0:
-            for copy in agg_out[0]:
-                copy.start()
+        for copy in agg_out[c]:
+            copy.start()
     for c in range(PARTS):
         agg_full[z, pl.ds(c * part, part)] = agg[
             pl.ds(pl.multiple_of(z1 * half + c * part, part), part), :
@@ -288,11 +287,6 @@
     in_sent[2].start()
     out_got[1].wait_recv()
     out_sent[2].start()
-    for c in range(1, PARTS):
-        for copy in agg_out[c - 1]:
-            copy.wait_send()
-        for copy in agg_out[c]:
-            copy.start()
     lax.fori_loop(cut, 5 * row_blocks, fill_dense, 0)
     tile = 256
 
@@ -533,7 +527,7 @@
 
     upd_out = pltpu.make_async_copy(upd_ref, upd_hbm, loc_sem.at[7])
     upd_out.start()
-    for copy in cot_out + in_sent + out_sent + agg_out[-1] + out_sends + [f_sib]:
+    for copy in cot_out + in_sent + out_sent + agg_out[0] + agg_out[1] + out_sends + [f_sib]:
         copy.wait_send()
     late = list(starts) + [(fwd_out, f_fwd), (passing, f_on)]
     for c_help, c_own, moves in p5_sent:

time: 110 us -> 106 us (0.964)
  Pallas kernels: 108 us -> 105 us
    pallas_call x1, Pallas kernels: 106 us -> 103 us  [body(): pl.pallas_call(functools.partial(kernel, n_row, n_rep), out_shape=(jax.Sh...]
where the time goes in v5:
time: 106 us; the launch traced here: 105 us
  Pallas kernels  105 us (99%)
    pallas_call x1, Pallas kernels, body(): pl.pallas_call(functools.partial(kernel, n_row, n_rep), out_shape=(jax.Sh...  103 us

profile of v5, /device:TPU:19, one launch (start us, length us, event | category | flops | bytes accessed | tf_op | source)
XLA Modules:
  0.0 105.3 jit_solution(10469869388441600244)
XLA Ops:
  0.6 102.6 %shard_map.77 = (bf16[1024,256]{1,0:T(8,128)(2,1)}, bf16[1024,256]{1,0:T(8,128)(2,1)}) custom-call(s32[4,8]{1,0:T(4,128)} %bitcast.3, s32[4,8]{1,0:T(4,128)} %bitcast.4, bf16[8,128,1024]{2,1,0:T(8,128)(2,1)} %bitcast.2, bf16[8,4,128,128]{3,2,1,0:T(8,128)(2,1)} %vals_ref.1, bf16[1024,1024]{1,0:T(8,128)(2,1)} %w_in_ref.1, bf16[1024,1024]{1,0:T(8,128)(2,1)} %w_out_ref.1, ...), custom_call_target="tpu_custom_call" | custom-call | tf_op jit(solution)/shard_map/pallas_call | solution.py:572
  103.2 2.1 %shard_map.78 = (bf16[1024,256]{1,0:T(8,128)(2,1)}, bf16[1024,256]{1,0:T(8,128)(2,1)}) custom-call(bf16[1024,256]{1,0:T(8,128)(2,1)} %get-tuple-element.4.upd_ref, bf16[1024,256]{1,0:T(8,128)(2,1)} %get-tuple-element.5.grad_ref), custom_call_target="tpu_custom_call" | custom-call | tf_op jit(solution)/shard_map/pallas_call | solution.py:621

commit v6 on v5

--- a/solution.py
+++ b/solution.py
@@ -30,9 +30,9 @@
 
 
 def kernel(
-    n_row, n_rep, cols_ref, spread_ref, feats_ref, vals_ref, w_in_ref, w_out_ref, cot_ref,
-    upd_hbm, grad_hbm,
-    upd_ref, grad_ref, ext, marks, vals, vals_t, dense_t, w1_in, w1_out, w2_in, w2_out, cot, cot_full, agg, agg_full, hid, gp,
+    n_row, n_rep, places_ref, feats_ref, vals_ref, w_in_ref, w_out_ref, cot_ref,
+    upd_ref, grad_ref,
+    cols_ref, spread_ref, ext, marks, vals, vals_t, dense_t, w1_in, w1_out, w2_in, w2_out, cot, cot_full, agg, agg_full, hid, gp,
     adj_p, out_p, adj_in, out_in, adj, c_send, c_sib, c_nbr, f_relay, c_relay,
     loc_sem, f_send, f_recv, w_send, w_recv, a_send, a_recv, c_sends, c_recvs, b_sends, b_recvs,
 ):
@@ -91,6 +91,8 @@
         for i, (src, dst) in enumerate(
             (
                 (vals_ref, vals),
+                (places_ref, cols_ref),
+                (places_ref, spread_ref),
                 (half_part(cot_ref, z1, 0, PARTS), cot_full.at[z]),
                 (w_in_ref, w1_in),
                 (w_out_ref, w1_out),
@@ -510,8 +512,6 @@
         turn(f)
     for f in range(WIDE):
         finish(f)
-    grad_out = pltpu.make_async_copy(grad_ref, grad_hbm, loc_sem.at[6])
-    grad_out.start()
     for c in range(PARTS):
         for copy in arrivals(out_in, 1 + (1 + WIDE) * PARTS + c, c):
             copy.wait_recv()
@@ -525,8 +525,6 @@
             at = pl.ds(s * half + c * part, part)
             upd_ref[at] = (mine.astype(F32) + total).astype(BF16)
 
-    upd_out = pltpu.make_async_copy(upd_ref, upd_hbm, loc_sem.at[7])
-    upd_out.start()
     for copy in cot_out + in_sent + out_sent + agg_out[0] + agg_out[1] + out_sends + [f_sib]:
         copy.wait_send()
     late = list(starts) + [(fwd_out, f_fwd), (passing, f_on)]
@@ -536,27 +534,21 @@
         late += list(moves)
     for ok, copy in late:
         pl.when(ok)(copy.wait_send)
-    grad_out.wait()
-    upd_out.wait()
-
-
-def settle(upd_ref, grad_ref, upd_out, grad_out, held, sems):
+
+
+def settle(upd_ref, grad_ref, upd_out, grad_out, sems):
     size = upd_ref.shape[0] // CUTS
-    steps = []
-    for i in range(CUTS):
-        rs = pl.ds(i * size, size)
-        for j, (src, dst) in enumerate(((upd_ref, upd_out), (grad_ref, grad_out))):
-            steps.append((
-                pltpu.make_async_copy(src.at[rs], held.at[j, rs], sems.at[0, j, i]),
-                pltpu.make_async_copy(held.at[j, rs], dst.at[rs], sems.at[1, j, i]),
-            ))
-    for load, _ in steps:
-        load.start()
-    for load, store in steps:
-        load.wait()
-        store.start()
-    for _, store in steps:
-        store.wait()
+    copies = [
+        pltpu.make_async_copy(
+            src.at[pl.ds(i * size, size)], dst.at[pl.ds(i * size, size)], sems.at[j, i]
+        )
+        for j, (src, dst) in enumerate(((upd_ref, upd_out), (grad_ref, grad_out)))
+        for i in range(CUTS)
+    ]
+    for copy in copies:
+        copy.start()
+    for copy in copies:
+        copy.wait()
 
 
 def body(n_row, n_rep, node_feats, block_cols, block_vals, w_in, w_out, cotangent):
@@ -571,12 +563,12 @@
     dma = pltpu.SemaphoreType.DMA
     made = pl.pallas_call(
         functools.partial(kernel, n_row, n_rep),
-        out_shape=(jax.ShapeDtypeStruct((rows, quarter), BF16),) * 2,
-        in_specs=[pl.BlockSpec(memory_space=pltpu.SMEM), vmem] + [anywhere] * 5,
-        out_specs=(anywhere, anywhere),
+        out_shape=(pltpu.VMEM((rows, quarter), BF16),) * 2,
+        in_specs=[anywhere] * 6,
+        out_specs=(vmem, vmem),
         scratch_shapes=[
-            pltpu.VMEM((rows, quarter), BF16),
-            pltpu.VMEM((rows, quarter), BF16),
+            pltpu.SMEM((slots, row_blocks), jnp.int32),
+            pltpu.VMEM((slots, row_blocks), jnp.int32),
             pltpu.VMEM((5 * row_blocks, 128, quarter), BF16),
             pltpu.VMEM((row_blocks * slots, 16, 128), jnp.int32),
             pltpu.VMEM((row_blocks, slots, 128, 128), BF16),
@@ -615,16 +607,16 @@
             dma((4 * WIDE,)),
         ],
         compiler_params=pltpu.CompilerParams(
-            collective_id=0, has_side_effects=True, vmem_limit_bytes=60 * 1024 * 1024
+            collective_id=0, has_side_effects=True, vmem_limit_bytes=56 * 1024 * 1024
         ),
-    )(block_cols.T, block_cols.T, node_feats.reshape(row_blocks, 128, feat), block_vals, w_in, w_out, cotangent)
+    )(block_cols.T, node_feats.reshape(row_blocks, 128, feat), block_vals, w_in, w_out, cotangent)
     return pl.pallas_call(
         settle,
         out_shape=(jax.ShapeDtypeStruct((rows, quarter), BF16),) * 2,
-        in_specs=[anywhere] * 2,
+        in_specs=[vmem] * 2,
         out_specs=(anywhere,) * 2,
-        scratch_shapes=[pltpu.VMEM((2, rows, quarter), BF16), dma((2, 2, CUTS))],
-    )(*made)
+        scratch_shapes=[dma((2, CUTS))],
+    )(*(pltpu.with_memory_space_constraint(m, pltpu.VMEM) for m in made))
 
 
 def solution(mesh):

time: 106 us -> 103 us (0.972)
  Pallas kernels: 105 us -> 102 us
    pallas_call x1, Pallas kernels: 103 us -> 101 us  [body(): pl.pallas_call(functools.partial(kernel, n_row, n_rep), out_shape=(pltpu....]
where the time goes in v6:
time: 103 us
  Pallas kernels  102 us (99%)
    pallas_call x1, Pallas kernels, body(): pl.pallas_call(functools.partial(kernel, n_row, n_rep), out_shape=(pltpu....  101 us

profile of v6, /device:TPU:19, one launch (start us, length us, event | category | flops | bytes accessed | tf_op | source)
XLA Modules:
  0.0 102.7 jit_solution(10967846303394178956)
XLA Ops:
  0.6 101.1 %shard_map.77 = (bf16[1024,256]{1,0:T(8,128)(2,1)S(1)}, bf16[1024,256]{1,0:T(8,128)(2,1)S(1)}) custom-call(s32[4,8]{1,0:T(4,128)} %bitcast.3, bf16[8,128,1024]{2,1,0:T(8,128)(2,1)} %bitcast.2, bf16[8,4,128,128]{3,2,1,0:T(8,128)(2,1)} %vals_ref.1, bf16[1024,1024]{1,0:T(8,128)(2,1)} %w_in_ref.1, bf16[1024,1024]{1,0:T(8,128)(2,1)} %w_out_ref.1, ...), custom_call_target="tpu_custom_call" | custom-call | tf_op jit(solution)/shard_map/pallas_call | solution.py:564
  101.7 1.0 %shard_map.78 = (bf16[1024,256]{1,0:T(8,128)(2,1)}, bf16[1024,256]{1,0:T(8,128)(2,1)}) custom-call(bf16[1024,256]{1,0:T(8,128)(2,1)S(1)} %get-tuple-element.4.upd_ref, bf16[1024,256]{1,0:T(8,128)(2,1)S(1)} %get-tuple-element.5.grad_ref), custom_call_target="tpu_custom_call" | custom-call | tf_op jit(solution)/shard_map/pallas_call | solution.py:613

commit v7 on v6

--- a/solution.py
+++ b/solution.py
@@ -32,7 +32,7 @@
 def kernel(
     n_row, n_rep, places_ref, feats_ref, vals_ref, w_in_ref, w_out_ref, cot_ref,
     upd_ref, grad_ref,
-    cols_ref, spread_ref, ext, marks, vals, vals_t, dense_t, w1_in, w1_out, w2_in, w2_out, cot, cot_full, agg, agg_full, hid, gp,
+    cols_ref, spread_ref, ext, marks, vals, vals_t, dense_t, w1_in, w1_out, w2_in, w2_out, cot, cot_full, agg, agg_full, hid, gp, gh,
     adj_p, out_p, adj_in, out_in, adj, c_send, c_sib, c_nbr, f_relay, c_relay,
     loc_sem, f_send, f_recv, w_send, w_recv, a_send, a_recv, c_sends, c_recvs, b_sends, b_recvs,
 ):
@@ -184,8 +184,9 @@
     in_sent[0].start()
     out_sent[0].start()
     cot_out = exchange(cot_ref, cot_full, 0, 0, PARTS)
-    for copy in cot_out:
-        copy.start()
+    outer = z1 == z2
+    for copy in cot_out[:2]:
+        pl.when(jnp.logical_not(outer))(copy.start)
 
     @pl.when(jnp.logical_not(has_dn))
     def _():
@@ -232,6 +233,15 @@
     def _():
         f_out.wait_recv()
         f_on.start()
+
+    in_sent[0].wait_send()
+    out_sent[0].wait_send()
+    for copy in cot_out[:2]:
+        pl.when(outer)(copy.start)
+    cot_out[2].start()
+    out_got[0].wait_recv()
+    out_sent[1].start()
+    in_got[0].wait_recv()
 
     @pl.when(has_dn)
     def _():
@@ -279,30 +289,38 @@
             pl.ds(pl.multiple_of(z1 * half + c * part, part), part), :
         ]
 
-    out_got[0].wait_recv()
-    out_sent[1].start()
-    in_got[0].wait_recv()
     in_sent[1].start()
-    cut = 3 * row_blocks
+    out_got[1].wait_recv()
+    out_sent[2].start()
+    cut = 2 * row_blocks
     lax.fori_loop(0, cut, fill_dense, 0)
     in_got[1].wait_recv()
     in_sent[2].start()
-    out_got[1].wait_recv()
-    out_sent[2].start()
     lax.fori_loop(cut, 5 * row_blocks, fill_dense, 0)
     tile = 256
 
-    def hidden_part(w_a, w_b, base, c):
+    def grad_part(w_b, base):
+        def step(i, carry):
+            hc = pl.ds(pl.multiple_of(i * tile, tile), tile)
+            to = pl.ds(pl.multiple_of(base + i * tile, tile), tile)
+            for c in range(PARTS):
+                rs = pl.ds(c * part, part)
+                g = jnp.concatenate([cot_full[q, rs] for q in range(n_rep)], axis=1)
+                gh[rs, to] = dot(g, w_b[:, hc])
+            return carry
+
+        lax.fori_loop(0, hidw // tile, step, 0)
+
+    def hidden_part(w_a, base, c):
         rs = pl.ds(c * part, part)
 
         def step(i, carry):
             hc = pl.ds(pl.multiple_of(i * tile, tile), tile)
             to = pl.ds(pl.multiple_of(base + i * tile, tile), tile)
             x = jnp.concatenate([agg_full[q, rs] for q in range(n_rep)], axis=1)
-            g = jnp.concatenate([cot_full[q, rs] for q in range(n_rep)], axis=1)
             value, slope = gelu_pair(dot(x, w_a[:, hc]))
             hid[rs, to] = value.astype(BF16)
-            gp[rs, to] = (dot(g, w_b[:, hc]) * slope).astype(BF16)
+            gp[rs, to] = (gh[rs, to] * slope).astype(BF16)
             return carry
 
         lax.fori_loop(0, hidw // tile, step, 0)
@@ -335,19 +353,20 @@
 
     for copy in arrivals(cot_full, 0, 0, PARTS):
         copy.wait_recv()
+    grad_part(w1_out, 0)
+    out_got[2].wait_recv()
+    out_sent[3].start()
+    in_got[2].wait_recv()
+    in_sent[3].start()
+    out_got[3].wait_recv()
+    grad_part(w2_out, hidw)
+    in_got[3].wait_recv()
     adj_sent = [[adj_copies(f, c) for c in range(PARTS)] for f in range(WIDE)]
     for c in range(PARTS):
         for copy in arrivals(agg_full, 1 + c, c):
             copy.wait_recv()
-        hidden_part(w1_in, w1_out, 0, c)
-        if c == 0:
-            in_got[2].wait_recv()
-            in_sent[3].start()
-            out_got[2].wait_recv()
-            out_sent[3].start()
-            in_got[3].wait_recv()
-            out_got[3].wait_recv()
-        hidden_part(w2_in, w2_out, hidw, c)
+        hidden_part(w1_in, 0, c)
+        hidden_part(w2_in, hidw, c)
         rs = pl.ds(c * part, part)
         for i, zp in enumerate(peers + [z]):
             res = product(gp, w1_in, w2_in, zp, c)
@@ -433,13 +452,12 @@
             (jnp.logical_and(helped_ok, jnp.logical_not(turn_helped)), c_helped[1]),
             (turning, c_out), (passing, c_on),
         )
-        put(1 + 2 * k, 0)
-        c_help.start()
         put(4 * k, 2)
-
         pl.when(turn_plain)(c_out.start)
         for ok, copy in moves[:2]:
             pl.when(ok)(copy.start)
+        put(1 + 2 * k, 0)
+        c_help.start()
         c_help.wait_recv()
 
         def add_help(m, carry):
@@ -453,13 +471,13 @@
         pl.when(turn_helped)(c_out.start)
         for ok, copy in moves[2:4]:
             pl.when(ok)(copy.start)
-        put(3 - 2 * k, 1)
-        c_own.start()
-
         @pl.when(passing)
         def _():
             c_out.wait_recv()
             c_on.start()
+
+        put(3 - 2 * k, 1)
+        c_own.start()
 
         p5_sent.append((c_help, c_own, moves))
 
@@ -525,7 +543,7 @@
             at = pl.ds(s * half + c * part, part)
             upd_ref[at] = (mine.astype(F32) + total).astype(BF16)
 
-    for copy in cot_out + in_sent + out_sent + agg_out[0] + agg_out[1] + out_sends + [f_sib]:
+    for copy in cot_out + in_sent[1:] + out_sent[1:] + agg_out[0] + agg_out[1] + out_sends + [f_sib]:
         copy.wait_send()
     late = list(starts) + [(fwd_out, f_fwd), (passing, f_on)]
     for c_help, c_own, moves in p5_sent:
@@ -584,6 +602,7 @@
             pltpu.VMEM((n_rep, half, quarter), BF16),
             pltpu.VMEM((half, 2 * hidw), BF16),
             pltpu.VMEM((half, 2 * hidw), BF16),
+            pltpu.VMEM((half, 2 * hidw), F32),
             pltpu.VMEM((n_rep, WIDE, half, width), BF16),
             pltpu.VMEM((n_rep, half, quarter), BF16),
             pltpu.VMEM((n_rep, WIDE, half, width), BF16),

time: 103 us -> 101 us (0.981)
  the two profiles are of different devices: /device:TPU:19 before, /device:TPU:16 now
where the time goes in v7:
time: 101 us
  Pallas kernels  100 us (99%)
    pallas_call x1, Pallas kernels, body(): pl.pallas_call(functools.partial(kernel, n_row, n_rep), out_shape=(pltpu....  99.3 us

profile of v7, /device:TPU:16, one launch (start us, length us, event | category | flops | bytes accessed | tf_op | source)
XLA Modules:
  0.0 100.9 jit_solution(11824952052313123819)
XLA Ops:
  0.6 99.3 %shard_map.77 = (bf16[1024,256]{1,0:T(8,128)(2,1)S(1)}, bf16[1024,256]{1,0:T(8,128)(2,1)S(1)}) custom-call(s32[4,8]{1,0:T(4,128)} %bitcast.3, bf16[8,128,1024]{2,1,0:T(8,128)(2,1)} %bitcast.2, bf16[8,4,128,128]{3,2,1,0:T(8,128)(2,1)} %vals_ref.1, bf16[1024,1024]{1,0:T(8,128)(2,1)} %w_in_ref.1, bf16[1024,1024]{1,0:T(8,128)(2,1)} %w_out_ref.1, ...), custom_call_target="tpu_custom_call" | custom-call | tf_op jit(solution)/shard_map/pallas_call | solution.py:582
  99.9 1.0 %shard_map.78 = (bf16[1024,256]{1,0:T(8,128)(2,1)}, bf16[1024,256]{1,0:T(8,128)(2,1)}) custom-call(bf16[1024,256]{1,0:T(8,128)(2,1)S(1)} %get-tuple-element.4.upd_ref, bf16[1024,256]{1,0:T(8,128)(2,1)S(1)} %get-tuple-element.5.grad_ref), custom_call_target="tpu_custom_call" | custom-call | tf_op jit(solution)/shard_map/pallas_call | solution.py:632

commit v8 on v7

--- a/solution.py
+++ b/solution.py
@@ -297,7 +297,7 @@
     in_got[1].wait_recv()
     in_sent[2].start()
     lax.fori_loop(cut, 5 * row_blocks, fill_dense, 0)
-    tile = 256
+    tile = 512
 
     def grad_part(w_b, base):
         def step(i, carry):

time: 101 us -> 101 us (level)
  the two profiles are of different devices: /device:TPU:16 before, /device:TPU:21 now
where the time goes in v8:
time: 101 us; the launch traced here: 100 us
  Pallas kernels  99.8 us (99%)
    pallas_call x1, Pallas kernels, body(): pl.pallas_call(functools.partial(kernel, n_row, n_rep), out_shape=(pltpu....  98.7 us

profile of v8, /device:TPU:21, one launch (start us, length us, event | category | flops | bytes accessed | tf_op | source)
XLA Modules:
  0.0 100.4 jit_solution(14688110270670839577)
XLA Ops:
  0.6 98.7 %shard_map.77 = (bf16[1024,256]{1,0:T(8,128)(2,1)S(1)}, bf16[1024,256]{1,0:T(8,128)(2,1)S(1)}) custom-call(s32[4,8]{1,0:T(4,128)} %bitcast.3, bf16[8,128,1024]{2,1,0:T(8,128)(2,1)} %bitcast.2, bf16[8,4,128,128]{3,2,1,0:T(8,128)(2,1)} %vals_ref.1, bf16[1024,1024]{1,0:T(8,128)(2,1)} %w_in_ref.1, bf16[1024,1024]{1,0:T(8,128)(2,1)} %w_out_ref.1, ...), custom_call_target="tpu_custom_call" | custom-call | tf_op jit(solution)/shard_map/pallas_call | solution.py:582
  99.4 1.0 %shard_map.78 = (bf16[1024,256]{1,0:T(8,128)(2,1)}, bf16[1024,256]{1,0:T(8,128)(2,1)}) custom-call(bf16[1024,256]{1,0:T(8,128)(2,1)S(1)} %get-tuple-element.4.upd_ref, bf16[1024,256]{1,0:T(8,128)(2,1)S(1)} %get-tuple-element.5.grad_ref), custom_call_target="tpu_custom_call" | custom-call | tf_op jit(solution)/shard_map/pallas_call | solution.py:632

commit v9 on v8

--- a/solution.py
+++ b/solution.py
@@ -297,7 +297,7 @@
     in_got[1].wait_recv()
     in_sent[2].start()
     lax.fori_loop(cut, 5 * row_blocks, fill_dense, 0)
-    tile = 512
+    tile = 1024
 
     def grad_part(w_b, base):
         def step(i, carry):

time: 101 us -> 99.5 us (0.985)
  the two profiles are of different devices: /device:TPU:21 before, /device:TPU:19 now
where the time goes in v9:
time: 99.5 us; the launch traced here: 97.6 us
  Pallas kernels  97 us (97%)
    pallas_call x1, Pallas kernels, body(): pl.pallas_call(functools.partial(kernel, n_row, n_rep), out_shape=(pltpu....  95.9 us

profile of v9, /device:TPU:19, one launch (start us, length us, event | category | flops | bytes accessed | tf_op | source)
XLA Modules:
  0.0 97.6 jit_solution(6521589747867221971)
XLA Ops:
  0.6 95.9 %shard_map.77 = (bf16[1024,256]{1,0:T(8,128)(2,1)S(1)}, bf16[1024,256]{1,0:T(8,128)(2,1)S(1)}) custom-call(s32[4,8]{1,0:T(4,128)} %bitcast.3, bf16[8,128,1024]{2,1,0:T(8,128)(2,1)} %bitcast.2, bf16[8,4,128,128]{3,2,1,0:T(8,128)(2,1)} %vals_ref.1, bf16[1024,1024]{1,0:T(8,128)(2,1)} %w_in_ref.1, bf16[1024,1024]{1,0:T(8,128)(2,1)} %w_out_ref.1, ...), custom_call_target="tpu_custom_call" | custom-call | tf_op jit(solution)/shard_map/pallas_call | solution.py:582
  96.6 1.0 %shard_map.78 = (bf16[1024,256]{1,0:T(8,128)(2,1)}, bf16[1024,256]{1,0:T(8,128)(2,1)}) custom-call(bf16[1024,256]{1,0:T(8,128)(2,1)S(1)} %get-tuple-element.4.upd_ref, bf16[1024,256]{1,0:T(8,128)(2,1)S(1)} %get-tuple-element.5.grad_ref), custom_call_target="tpu_custom_call" | custom-call | tf_op jit(solution)/shard_map/pallas_call | solution.py:632
